TPU v7x, 512 devices: a whole 4x8x8 slice. The times are simulated.
512 devices in a mesh: dom: 128 (over y, z, core), edge: 4 (over x).
Axes of the slice: x: 4, y: 8, z: 8, core: 2. Of those that a mesh axis runs over, the one named last changes fastest.
Arguments:
- node_feat: bfloat16 [32768, 512], P('dom'), may hold values from -6 to 6
- edge_feat: bfloat16 [262144, 512], P(('dom', 'edge')), may hold values from -6 to 6
- edge_slot: int32 [262144], P(('dom', 'edge')), may hold values from 0 to 2303, as said below
- edge_recv: int32 [262144], P(('dom', 'edge')), may hold values from 0 to 255
- send_list: int32 [128, 128, 16], P('dom'), may hold values from 0 to 255
- edge_w_edge: bfloat16 [512, 512], P('edge'), may hold values from -0.15625 to 0.15625
- edge_w_send: bfloat16 [512, 512], P('edge'), may hold values from -0.15625 to 0.15625
- edge_w_recv: bfloat16 [512, 512], P('edge'), may hold values from -0.15625 to 0.15625
- edge_w_out: bfloat16 [512, 512], P('edge'), may hold values from -0.25 to 0.25
- edge_gain: float32 [512], replicated, may hold values from 0.5 to 1.5
- node_w_self: bfloat16 [512, 512], P('edge'), may hold values from -0.1875 to 0.1875
- node_w_agg: bfloat16 [512, 512], P('edge'), may hold values from -0.1875 to 0.1875
- node_w_out: bfloat16 [512, 512], P('edge'), may hold values from -0.25 to 0.25
- node_gain: float32 [512], replicated, may hold values from 0.5 to 1.5
Outputs:
- node_out: bfloat16 [32768, 512], P('dom')
- edge_out: bfloat16 [262144, 512], P(('dom', 'edge'))
Inputs may be any that keep to these rules, and one draw needn't show every extreme that they name: `edge_slot`: A value v >= 256 of an edge of partition p names a slot u % 16 of the list of partition u // 16 for p, with u = v - 256; that partition is never p.
All inputs are finite; a program needn't handle non-finite values.
Results may differ from a plain program's by a relative error of at most 0.018.
Values may be sent and summed in bfloat16 or wider, within the bound.
No kernel may reach another device: no remote copies, remote signals or barrier semaphores. Data moves between devices by JAX's collectives and lax.ppermute only.
A program may use at most 64 MiB of HBM per device.

v0:
```python
import jax
import jax.numpy as jnp
from jax import lax
from jax.sharding import PartitionSpec as P


def layer_normalize(values):
    center = values - jnp.mean(values, axis=-1, keepdims=True)
    spread = jnp.mean(center * center, axis=-1, keepdims=True)
    return center * lax.rsqrt(spread + 1e-05)


def node_finish(node_rows_in, node_pre, w_out_node, node_gain):
    node_hidden = jax.nn.silu(node_pre).astype(jnp.bfloat16)
    node_update = (
        layer_normalize(jnp.dot(node_hidden, w_out_node, preferred_element_type=jnp.float32))
        * node_gain
    )
    return (node_rows_in.astype(jnp.float32) + node_update).astype(jnp.bfloat16)


def local(
    node_feat,
    edge_feat,
    edge_slot,
    edge_recv,
    send_list,
    edge_w_edge,
    edge_w_send,
    edge_w_recv,
    edge_w_out,
    edge_gain,
    node_w_self,
    node_w_agg,
    node_w_out,
    node_gain,
):
    group_size = lax.axis_size("edge")
    member = lax.axis_index("edge")
    node_rows, feat_width = node_feat.shape
    column_share = feat_width // group_size
    w_edge, w_send, w_recv, w_out_edge, w_out_node = (
        lax.all_gather(edge_w_edge, "edge", axis=0, tiled=True),
        lax.all_gather(edge_w_send, "edge", axis=0, tiled=True),
        lax.all_gather(edge_w_recv, "edge", axis=0, tiled=True),
        lax.all_gather(edge_w_out, "edge", axis=0, tiled=True),
        lax.all_gather(node_w_out, "edge", axis=0, tiled=True),
    )
    listed = send_list[0]
    peer_count, slot_count = listed.shape
    listed_rows = listed.reshape(-1)
    outgoing = jnp.take(node_feat, listed_rows, axis=0).reshape(peer_count, slot_count, feat_width)
    arrived = lax.all_to_all(outgoing, "dom", split_axis=0, concat_axis=0, tiled=True)
    remote = arrived.reshape(peer_count * slot_count, feat_width)
    table = jnp.concatenate([node_feat, remote], axis=0)
    senders = jnp.take(table, edge_slot, axis=0)
    node_ids = jnp.arange(node_rows, dtype=jnp.int32)
    onehot = (node_ids[:, None] == edge_recv[None, :]).astype(jnp.bfloat16)
    receivers = lax.dot_general(
        onehot, node_feat, (((0,), (0,)), ((), ())), preferred_element_type=jnp.float32
    ).astype(jnp.bfloat16)
    edge_pre = jnp.dot(edge_feat, w_edge, preferred_element_type=jnp.float32)
    edge_pre = edge_pre + jnp.dot(senders, w_send, preferred_element_type=jnp.float32)
    edge_pre = edge_pre + jnp.dot(receivers, w_recv, preferred_element_type=jnp.float32)
    edge_hidden = jax.nn.silu(edge_pre).astype(jnp.bfloat16)
    message = (
        layer_normalize(jnp.dot(edge_hidden, w_out_edge, preferred_element_type=jnp.float32))
        * edge_gain
    )
    edge_out = (edge_feat.astype(jnp.float32) + message).astype(jnp.bfloat16)
    message_high = message.astype(jnp.bfloat16)
    message_low = (message - message_high.astype(jnp.float32)).astype(jnp.bfloat16)
    partial_total = jnp.dot(onehot, message_high, preferred_element_type=jnp.float32) + jnp.dot(
        onehot, message_low, preferred_element_type=jnp.float32
    )
    share_total = lax.psum_scatter(
        partial_total.astype(jnp.bfloat16), "edge", scatter_dimension=1, tiled=True
    )
    self_columns = lax.dynamic_slice_in_dim(node_feat, member * column_share, column_share, 1)
    partial_pre = jnp.dot(self_columns, node_w_self, preferred_element_type=jnp.float32)
    partial_pre = partial_pre + jnp.dot(share_total, node_w_agg, preferred_element_type=jnp.float32)
    node_pre = lax.psum(partial_pre.astype(jnp.bfloat16), "edge").astype(jnp.float32)
    node_out = node_finish(node_feat, node_pre, w_out_node, node_gain)
    return (node_out, edge_out)


def solution(mesh):
    in_specs = (
        P("dom", None),
        P(("dom", "edge"), None),
        P(("dom", "edge")),
        P(("dom", "edge")),
        P("dom", None, None),
        P("edge", None),
        P("edge", None),
        P("edge", None),
        P("edge", None),
        P(),
        P("edge", None),
        P("edge", None),
        P("edge", None),
        P(),
    )
    out_specs = (P("dom", None), P(("dom", "edge"), None))
    return jax.shard_map(local, mesh=mesh, in_specs=in_specs, out_specs=out_specs, check_vma=False)
```

profile of v0, /device:TPU:56, one launch (start us, length us, event | category | flops | bytes accessed | tf_op | source)
XLA Modules:
  0.0 193.1 jit_solution(2516224030115538195)
XLA Ops:
  7.2 0.0 copy-start
  7.2 0.8 copy.24
  8.0 0.7 compare_and_fusion
  8.7 0.1 reshape_squeeze.6
  8.8 0.1 copy.23
  9.0 8.6 %gather_fusion = bf16[2048,512]{1,0:T(8,128)(2,1)S(1)} fusion(bf16[256,512]{1,0:T(8,128)(2,1)} %param.14, s32[2048]{0:T(1024)S(1)} %broadcast_clamp_fusion), kind=kCustom, calls=%fused_computation | custom fusion | bytes 4202496 | tf_op jit(solution)/shard_map/jit(_take)/gather | solution.py:52
  17.5 1.6 broadcast_select_fusion
  19.1 0.0 copy-start.9
  19.1 17.5 %all-to-all-start = ((bf16[128,16,512]{2,1,0:T(8,128)(2,1)}), bf16[128,16,512]{2,1,0:T(8,128)(2,1)S(1)}, u32[]{:S(2)}, u32[]{:S(2)}) async-start(bf16[128,16,512]{2,1,0:T(8,128)(2,1)} %broadcast_select_fusion), calls=%async_computation | async-start | bytes 4194304 | tf_op jit(solution)/shard_map/all_to_all | solution.py:53
  36.6 0.0 reduce-scatter.4.cloned.1.call-start
  36.7 0.0 copy-done.13
  36.7 0.0 copy-start.3
  36.7 0.0 copy-done.6
  36.7 13.3 %all_gather.15 = bf16[512,512]{1,0:T(8,128)(2,1)S(1)} all-gather(bf16[128,512]{1,0:T(8,128)(2,1)S(1)} %copy-done.6), channel_id=1, replica_groups=mesh['dom'=128,'edge'=4] {'edge'}, dimensions={0}, use_global_device_ids=true | all-gather | bytes 655360 | tf_op jit(solution)/shard_map/all_gather | solution.py:43
  50.0 14.1 %all_gather.16 = bf16[512,512]{1,0:T(8,128)(2,1)} all-gather(bf16[128,512]{1,0:T(8,128)(2,1)S(1)} %copy-done.7), channel_id=1, replica_groups=mesh['dom'=128,'edge'=4] {'edge'}, dimensions={0}, use_global_device_ids=true | all-gather | bytes 655360 | tf_op jit(solution)/shard_map/all_gather | solution.py:44
  64.1 13.8 %all_gather.17 = bf16[512,512]{1,0:T(8,128)(2,1)} all-gather(bf16[128,512]{1,0:T(8,128)(2,1)S(1)} %copy-done.8), channel_id=1, replica_groups=mesh['dom'=128,'edge'=4] {'edge'}, dimensions={0}, use_global_device_ids=true | all-gather | bytes 655360 | tf_op jit(solution)/shard_map/all_gather | solution.py:45
  77.9 0.0 copy-done.9
  77.9 12.8 %all_gather.18 = bf16[512,512]{1,0:T(8,128)(2,1)S(1)} all-gather(bf16[128,512]{1,0:T(8,128)(2,1)S(1)} %copy-done.9), channel_id=1, replica_groups=mesh['dom'=128,'edge'=4] {'edge'}, dimensions={0}, use_global_device_ids=true | all-gather | bytes 655360 | tf_op jit(solution)/shard_map/all_gather | solution.py:46
  90.7 1.4 fusion.33
  92.1 0.0 all-to-all-done
  92.1 1.3 copy-done.2
  93.5 1.7 pad_maximum_fusion
  95.2 2.6 %gather_fusion.1 = bf16[512,512]{1,0:T(8,128)(2,1)} fusion(bf16[2304,512]{1,0:T(8,128)(2,1)S(1)} %pad_maximum_fusion, s32[1024]{0:T(1024)S(1)} %pad_clamp_fusion), kind=kCustom, calls=%fused_computation.1 | custom fusion | bytes 1050624 | tf_op jit(solution)/shard_map/jit(_take)/gather | solution.py:56
  97.9 2.1 %convolution_add_fusion.1 = f32[512,512]{1,0:T(8,128)S(1)} fusion(f32[512,512]{1,0:T(8,128)} %fusion.33, bf16[512,512]{1,0:T(8,128)(2,1)} %all_gather.16, bf16[512,512]{1,0:T(8,128)(2,1)} %gather_fusion.1, pred[512]{0:T(512)(128)(4,1)S(1)} %compare_and_fusion.1), kind=kOutput, calls=%fused_computation.5 | convolution fusion | flops 268959744 | bytes 3146240 | tf_op jit(solution)/shard_map/dot_general | solution.py:63
  100.0 0.8 multiply_convert_fusion
  100.8 0.0 copy-start.12
  100.8 0.5 fusion.31
  101.3 0.2 multiply_reduce_fusion
  101.5 0.0 copy-start.4
  101.5 0.4 fusion.3
  101.9 0.0 copy-start.10
  101.9 0.4 fusion
  102.4 0.0 copy-start.11
  102.4 0.8 copy.27
  103.2 0.0 reduce-scatter.4.cloned.1.call-update
  103.3 0.0 all-reduce.2.cloned.1.call-start
  103.3 0.2 copy.25
  103.5 12.8 %all_gather.19 = bf16[512,512]{1,0:T(8,128)(2,1)S(1)} all-gather(bf16[128,512]{1,0:T(8,128)(2,1)S(1)} %copy-done.10), channel_id=1, replica_groups=mesh['dom'=128,'edge'=4] {'edge'}, dimensions={0}, use_global_device_ids=true | all-gather | bytes 655360 | tf_op jit(solution)/shard_map/all_gather | solution.py:47
  116.3 0.2 fusion.26
  116.5 12.1 %reduce-scatter.4.cloned.1.call-done = bf16[128,256]{1,0:T(8,128)(2,1)} async-done(((bf16[512,256]{1,0:T(8,128)(2,1)}), bf16[128,256]{1,0:T(8,128)(2,1)}) %reduce-scatter.4.cloned.1.call-update) | async-done | bytes 65552
  128.6 1.8 fusion.1
  130.4 0.0 all-reduce.2.cloned.1.call-update
  130.4 0.2 add_convert_fusion
  130.6 1.0 copy.26
  131.6 52.1 %all-reduce.2.cloned.1.call-done = bf16[256,512]{1,0:T(8,128)(2,1)} async-done(((bf16[256,512]{1,0:T(8,128)(2,1)}), bf16[256,512]{1,0:T(8,128)(2,1)}) %all-reduce.2.cloned.1.call-update) | async-done | bytes 262160 | tf_op jit(solution)/shard_map/psum | solution.py:82
  183.8 1.4 fusion.32
  185.2 0.2 multiply_reduce_fusion.1
  185.4 0.9 add_convert_fusion.1
  (30 shorter events, 0.1 us)
Async XLA Ops:
  7.2 109.2 %copy-start = (bf16[128,512]{1,0:T(8,128)(2,1)S(1)}, bf16[128,512]{1,0:T(8,128)(2,1)}, u32[]{:S(2)}) copy-start(bf16[128,512]{1,0:T(8,128)(2,1)} %param.24) | copy-start | bytes 393220
  19.1 17.6 %copy-start.13 = (s32[512]{0:T(512)S(1)}, s32[512]{0:T(512)}, u32[]{:S(2)}) copy-start(s32[512]{0:T(512)} %param.16) | copy-start | bytes 6148
  19.1 17.6 %copy-start.6 = (bf16[128,512]{1,0:T(8,128)(2,1)S(1)}, bf16[128,512]{1,0:T(8,128)(2,1)}, u32[]{:S(2)}) copy-start(bf16[128,512]{1,0:T(8,128)(2,1)} %param.19) | copy-start | bytes 393220
  19.1 30.9 %copy-start.7 = (bf16[128,512]{1,0:T(8,128)(2,1)S(1)}, bf16[128,512]{1,0:T(8,128)(2,1)}, u32[]{:S(2)}) copy-start(bf16[128,512]{1,0:T(8,128)(2,1)} %param.20) | copy-start | bytes 393220
  19.1 45.0 %copy-start.8 = (bf16[128,512]{1,0:T(8,128)(2,1)S(1)}, bf16[128,512]{1,0:T(8,128)(2,1)}, u32[]{:S(2)}) copy-start(bf16[128,512]{1,0:T(8,128)(2,1)} %param.21) | copy-start | bytes 393220
  19.1 58.8 %copy-start.9 = (bf16[128,512]{1,0:T(8,128)(2,1)S(1)}, bf16[128,512]{1,0:T(8,128)(2,1)}, u32[]{:S(2)}) copy-start(bf16[128,512]{1,0:T(8,128)(2,1)} %param.22) | copy-start | bytes 393220
  19.1 73.0 %all-to-all-start = ((bf16[128,16,512]{2,1,0:T(8,128)(2,1)}), bf16[128,16,512]{2,1,0:T(8,128)(2,1)S(1)}, u32[]{:S(2)}, u32[]{:S(2)}) async-start(bf16[128,16,512]{2,1,0:T(8,128)(2,1)} %broadcast_select_fusion), calls=%async_computation | async-start | bytes 4194304 | tf_op jit(solution)/shard_map/all_to_all | solution.py:53
  36.6 92.0 %reduce-scatter.4.cloned.1.call-start = ((), (), s32[]{:S(2)}) async-start(), calls=%async_computation.3 | async-start | bytes 327680
  36.7 54.0 %copy-start.3 = (bf16[512,512]{1,0:T(8,128)(2,1)S(1)}, bf16[512,512]{1,0:T(8,128)(2,1)}, u32[]{:S(2)}) copy-start(bf16[512,512]{1,0:T(8,128)(2,1)} %param.15) | copy-start | bytes 1572868
  50.0 43.5 %copy-start.1 = (bf16[256,512]{1,0:T(8,128)(2,1)S(1)}, bf16[256,512]{1,0:T(8,128)(2,1)}, u32[]{:S(2)}) copy-start(bf16[256,512]{1,0:T(8,128)(2,1)} %param.14) | copy-start | bytes 786436
  92.1 1.3 copy-start.2
  97.9 2.1 %copy-start.5 = (bf16[512,512]{1,0:T(8,128)(2,1)S(1)}, bf16[512,512]{1,0:T(8,128)(2,1)}, u32[]{:S(2)}) copy-start(bf16[512,512]{1,0:T(8,128)(2,1)} %all_gather.17) | copy-start | bytes 1572868
  97.9 2.1 %copy-start.14 = (s32[512]{0:T(512)S(1)}, s32[512]{0:T(512)}, u32[]{:S(2)}) copy-start(s32[512]{0:T(512)} %param.17) | copy-start | bytes 6148
  100.8 0.7 copy-start.12
  101.5 1.8 copy-start.4
  101.9 1.6 copy-start.10
  102.4 26.2 %copy-start.11 = (bf16[128,512]{1,0:T(8,128)(2,1)S(1)}, bf16[128,512]{1,0:T(8,128)(2,1)}, u32[]{:S(2)}) copy-start(bf16[128,512]{1,0:T(8,128)(2,1)} %param.25) | copy-start | bytes 393220
  103.3 80.5 %all-reduce.2.cloned.1.call-start = ((), (), s32[]{:S(2)}) async-start(), calls=%async_computation.2 | async-start | bytes 524288 | tf_op jit(solution)/shard_map/psum | solution.py:82
  131.6 53.7 %copy-start.15 = (f32[512]{0:T(512)S(1)}, f32[512]{0:T(512)}, u32[]{:S(2)}) copy-start(f32[512]{0:T(512)} %param.27) | copy-start | bytes 6148
Sparse Core Ops, SparseCore 0:
  103.4 25.1 reduce-scatter.3
  131.6 52.1 all-reduce.1
where the time goes:
time: 194 us; the launch traced here: 193 us
  blocking collectives  66.7 us (34%)
  waiting for transfers between devices  64.2 us (33%)
  starting transfers between devices  17.6 us (9%)
  local copies, waits for them, and re-layouts  15.7 us (8%)
  between operations  14.3 us (7%)
  matrix products  8.98 us (5%)
  other arithmetic  5.57 us (3%)
    psum x1, waiting for transfers between devices, local(): lax.psum(partial_pre.astype(jnp.bfloat16), 'edge').astype(jnp.float32)  52.1 us
    all_to_all x1, starting transfers between devices, local(): lax.all_to_all(outgoing, 'dom', split_axis=0, concat_axis=0, tiled=True)  17.5 us
    all_gather x1, blocking collectives, local(): lax.all_gather(edge_w_send, 'edge', axis=0, tiled=True)  14.1 us
    all_gather x1, blocking collectives, local(): lax.all_gather(edge_w_recv, 'edge', axis=0, tiled=True)  13.8 us
    all_gather x1, blocking collectives, local(): lax.all_gather(edge_w_edge, 'edge', axis=0, tiled=True)  13.3 us
    all_gather x1, blocking collectives, local(): lax.all_gather(node_w_out, 'edge', axis=0, tiled=True)  12.8 us
    all_gather x1, blocking collectives, local(): lax.all_gather(edge_w_out, 'edge', axis=0, tiled=True)  12.8 us
    unnamed x3, waiting for transfers between devices  12.1 us
  transfers between devices with their start and end apart: 3, of which 2 were waited for; matrix products, arithmetic and copies ran while one was open for 2% of the time, Pallas kernels for 0%

commit v1 on v0

v1 whole, which is shorter than its diff:
```python
import functools

import jax
import jax.numpy as jnp
from jax import lax
from jax.experimental import pallas as pl
from jax.experimental.pallas import tpu as pltpu
from jax.sharding import PartitionSpec as P

F32 = jnp.float32
BF16 = jnp.bfloat16
LANE = 128
VMEM_BYTES = 40 * 1024 * 1024

W_EDGE, W_RECV, W_SEND, W_OUT, W_AGG, W_NODE = range(6)
HALF = 3


def whole(*shape):
    return pl.BlockSpec(shape, lambda i: (0,) * len(shape))


def one_of(index, *shape):
    return pl.BlockSpec((None,) + shape, lambda i: (index,) + (0,) * len(shape))


def call(body, outs, in_specs, flops, nbytes, scratch=(), out_specs=None):
    return pl.pallas_call(
        body,
        out_shape=outs,
        grid=(1,),
        in_specs=in_specs,
        out_specs=out_specs
        if out_specs is not None
        else jax.tree.map(lambda o: whole(*o.shape), outs),
        scratch_shapes=scratch,
        compiler_params=pltpu.CompilerParams(vmem_limit_bytes=VMEM_BYTES),
        cost_estimate=pl.CostEstimate(flops=flops, bytes_accessed=nbytes, transcendentals=0),
    )


def silu(v):
    return 0.5 * v * (1.0 + jnp.tanh(0.5 * v))


def normalize(v):
    center = v - jnp.mean(v, axis=-1, keepdims=True)
    spread = jnp.mean(center * center, axis=-1, keepdims=True)
    return center * lax.rsqrt(spread + 1e-05)


def dot(a, b):
    return jnp.dot(a, b, preferred_element_type=F32)


def shard_order():
    x = lax.axis_index("edge")
    core = lax.rem(lax.axis_index("dom"), 2)
    step = jnp.where(core == 0, 3, 1)
    return (x, lax.rem(x + step, 4), lax.rem(x + 4 - step, 4), lax.rem(x + 2, 4))


def columns(j):
    return pl.ds(pl.multiple_of(j * LANE, LANE), LANE)


def by_shard(ref, rows, order):
    return jnp.concatenate([ref[rows, columns(j)] for j in order], axis=1)


def stacked(refs):
    return jnp.concatenate([r[...] for r in refs], axis=0)


def column_of(row_block):
    return jnp.transpose(row_block.astype(F32))


def pack_kernel(*refs):
    shards, (packed, half, sem) = refs[:6], refs[6:]
    core = lax.rem(lax.axis_index("dom"), 2)
    copies = [pltpu.make_async_copy(s, packed.at[k], sem.at[k]) for k, s in enumerate(shards)]
    for c in copies:
        c.start()
    for side in range(2):
        @pl.when(core == side)
        def _():
            mine = [
                pltpu.make_async_copy(shards[HALF * side + k], half.at[k], sem.at[6 + k])
                for k in range(HALF)
            ]
            for c in mine:
                c.start()
            for c in mine:
                c.wait()
    for c in copies:
        c.wait()


def pick_kernel(listed_ref, node_ref, out_ref):
    slots, peers = listed_ref.shape
    nodes = node_ref.shape[0]
    mine = node_ref[:, columns(lax.axis_index("edge"))]
    listed = listed_ref[...].astype(F32).astype(BF16)
    rows = min(512, peers * slots)
    shift = slots.bit_length() - 1
    ones = jnp.ones((slots, nodes), BF16)
    for base in range(0, peers * slots, rows):
        place = base + lax.broadcasted_iota(jnp.int32, (rows, peers), 0)
        peer = lax.broadcasted_iota(jnp.int32, (rows, peers), 1)
        spread = jnp.where(lax.shift_right_logical(place, shift) == peer, 1.0, 0.0).astype(BF16)
        found = lax.dot_general(
            spread, listed, (((1,), (1,)), ((), ())), preferred_element_type=F32
        )
        slot = jnp.bitwise_and(lax.broadcasted_iota(jnp.int32, (rows, slots), 0), slots - 1)
        lane = lax.broadcasted_iota(jnp.int32, (rows, slots), 1)
        found = jnp.where(slot == lane, found, 0.0).astype(BF16)
        wanted = dot(found, ones)
        node = lax.broadcasted_iota(jnp.int32, (rows, nodes), 1).astype(F32)
        onehot = jnp.where(wanted == node, 1.0, 0.0).astype(BF16)
        out_ref[base : base + rows, :] = dot(onehot, mine).astype(BF16)


def choose_kernel(nodes, own_ref, left_ref, right_ref, far_ref, table_ref, out_ref):
    x = lax.axis_index("edge")
    entries = table_ref.shape[0]
    width = 256
    lane = lax.broadcasted_iota(jnp.int32, (LANE, width), 1).astype(F32)
    for ref, away in ((own_ref, 0), (left_ref, 3), (right_ref, 1), (far_ref, 2)):
        wanted = column_of(ref[...] - nodes)
        blocks = []
        for g in range(ref.shape[0]):
            total = jnp.zeros((LANE, LANE), F32)
            for base in range(0, entries, width):
                w = min(width, entries - base)
                onehot = jnp.where(
                    wanted[:, g : g + 1] - float(base) == lane[:, :w], 1.0, 0.0
                ).astype(BF16)
                total = total + dot(onehot, table_ref[base : base + w, :])
            blocks.append(total.astype(BF16))
        out_ref[lax.rem(x + away, 4), :, :] = jnp.concatenate(blocks, axis=1)


def base_kernel(
    edge_ref, node_ref, slot_ref, recv_ref,
    e0, e1, e2, e3, r0, r1, r2, r3, s0, s1, s2, s3, base_ref, table_ref,
):
    order = shard_order()
    nodes = node_ref.shape[0]
    by_node = by_shard(node_ref, slice(None), order)
    table_ref[0] = dot(by_node, stacked((s0, s1, s2, s3))).astype(BF16)
    table_ref[1] = dot(by_node, stacked((r0, r1, r2, r3))).astype(BF16)
    w_edge = stacked((e0, e1, e2, e3))
    slot = column_of(slot_ref[...])
    recv = column_of(recv_ref[...])
    lane = lax.broadcasted_iota(jnp.int32, (LANE, nodes), 1).astype(F32)
    for g in range(slot_ref.shape[0]):
        rows = slice(g * LANE, (g + 1) * LANE)
        from_slot = jnp.where(slot[:, g : g + 1] == lane, 1.0, 0.0).astype(BF16)
        from_recv = jnp.where(recv[:, g : g + 1] == lane, 1.0, 0.0).astype(BF16)
        total = dot(by_shard(edge_ref, rows, order), w_edge)
        total = total + dot(from_slot, table_ref[0])
        base_ref[rows, :] = total + dot(from_recv, table_ref[1])


def edge_kernel(
    edge_ref, base_ref, got_ref, recv_ref, node_ref, self_ref, gain_ref,
    s0, s1, s2, s3, o0, o1, o2, o3, a0, a1, a2, a3,
    out_ref, term_ref, hidden_ref, message_ref, total_ref,
):
    order = shard_order()
    w_send = stacked((s0, s1, s2, s3))
    w_out = stacked((o0, o1, o2, o3))
    edges, width = edge_ref.shape
    for g in range(edges // LANE):
        rows = slice(g * LANE, (g + 1) * LANE)
        sender = jnp.concatenate([got_ref[j, :, g * LANE : (g + 1) * LANE] for j in order], axis=1)
        hidden = silu(base_ref[rows, :] + dot(sender, w_send)).astype(BF16)
        hidden_ref[rows, :] = hidden
    for g in range(edges // LANE):
        rows = slice(g * LANE, (g + 1) * LANE)
        message = normalize(dot(by_shard(hidden_ref, rows, order), w_out)) * gain_ref[...]
        out_ref[rows, :] = (edge_ref[rows, :].astype(F32) + message).astype(BF16)
        message_ref[rows, :] = message.astype(BF16)
    nodes = node_ref.shape[0]
    node = lax.broadcasted_iota(jnp.int32, (nodes, LANE), 0)
    onehot = jnp.concatenate(
        [
            jnp.where(recv_ref[g : g + 1, :] == node, 1.0, 0.0).astype(BF16)
            for g in range(edges // LANE)
        ],
        axis=1,
    )
    total_ref[...] = dot(onehot, message_ref[...]).astype(BF16)
    term = dot(by_shard(total_ref, slice(None), order), stacked((a0, a1, a2, a3)))
    own = node_ref[:, columns(lax.axis_index("edge"))]
    term = (term + dot(own, self_ref[...])).astype(BF16)
    for j in range(term_ref.shape[0]):
        term_ref[j] = term


def node_kernel(terms_ref, node_ref, gain_ref, n0, n1, n2, n3, out_ref, hidden_ref):
    order = shard_order()
    terms = [terms_ref[j].astype(F32) for j in range(terms_ref.shape[0])]
    hidden_ref[...] = silu((terms[0] + terms[1]) + (terms[2] + terms[3])).astype(BF16)
    update = normalize(
        dot(by_shard(hidden_ref, slice(None), order), stacked((n0, n1, n2, n3)))
    )
    out_ref[...] = (node_ref[...].astype(F32) + update * gain_ref[...]).astype(BF16)


def local(
    node_feat, edge_feat, edge_slot, edge_recv, send_list, edge_w_edge, edge_w_send, edge_w_recv,
    edge_w_out, edge_gain, node_w_self, node_w_agg, node_w_out, node_gain,
):
    peers = lax.axis_size("dom")
    core = lax.rem(lax.axis_index("dom"), 2)
    nodes, width = node_feat.shape
    edges = edge_feat.shape[0]
    part, hid = edge_w_edge.shape
    slots = send_list.shape[2]
    entries = peers * slots
    groups = edges // LANE
    weight = jax.ShapeDtypeStruct

    def ring(away):
        return [(i, (i + away) % 4) for i in range(4)]

    both = [
        (d * 4 + i, d * 4 + (i + (1 if d % 2 == 0 else 3)) % 4)
        for d in range(peers)
        for i in range(4)
    ]
    swap = [(d, d ^ 1) for d in range(peers)]

    with jax.named_scope("pick_listed"):
        outgoing = call(
            pick_kernel,
            weight((entries, LANE), BF16),
            [whole(slots, peers), whole(nodes, width)],
            2 * entries * 640 * LANE,
            entries * 256 + nodes * width * 2,
        )(send_list[0].T, node_feat)
    with jax.named_scope("send_listed"):
        arrived = lax.all_to_all(
            outgoing.reshape(peers, slots, LANE), "dom", split_axis=0, concat_axis=0, tiled=True
        )
    with jax.named_scope("pack_shards"):
        anywhere = pl.BlockSpec(memory_space=pl.ANY)
        own_w, own_half = call(
            pack_kernel,
            (weight((6, part, hid), BF16), weight((HALF, part, hid), BF16)),
            [anywhere] * 6,
            0,
            18 * part * hid * 2,
            scratch=[pltpu.SemaphoreType.DMA((9,))],
            out_specs=(anywhere, anywhere),
        )(edge_w_edge, edge_w_recv, edge_w_send, edge_w_out, node_w_agg, node_w_out)
    with jax.named_scope("send_shards"):
        near_w = lax.ppermute(own_w, ("dom", "edge"), both)
        far_half = lax.ppermute(own_half, "edge", ring(2))
        across_w = lax.ppermute(near_w, "dom", swap)
        across_half = lax.ppermute(far_half, "dom", swap)
        low_half = lax.select(core == 0, far_half, across_half)
        high_half = lax.select(core == 0, across_half, far_half)
    with jax.named_scope("send_slots"):
        own_slot = edge_slot.reshape(groups, LANE)
        left_slot = lax.ppermute(own_slot, "edge", ring(1))
        right_slot = lax.ppermute(own_slot, "edge", ring(3))
        far_slot = lax.ppermute(own_slot, "edge", ring(2))
    recv = edge_recv.reshape(groups, LANE)

    def weights(k):
        far = low_half if k < HALF else high_half
        specs = [one_of(k, part, hid)] * 3 + [one_of(k % HALF, part, hid)]
        return (own_w, near_w, across_w, far), specs

    with jax.named_scope("edge_pre_local"):
        args, specs = zip(*[weights(k) for k in (W_EDGE, W_RECV, W_SEND)])
        base = call(
            base_kernel,
            weight((edges, hid), F32),
            [whole(edges, width), whole(nodes, width), whole(groups, LANE), whole(groups, LANE)]
            + sum(specs, []),
            2 * (2 * edges + 2 * nodes) * width * hid,
            edges * width * 6 + 3 * width * hid * 2,
            scratch=[pltpu.VMEM((2, nodes, hid), BF16)],
        )(edge_feat, node_feat, own_slot, recv, *sum(args, ()))
    with jax.named_scope("choose_senders"):
        chosen = call(
            functools.partial(choose_kernel, nodes),
            weight((4, LANE, groups * LANE), BF16),
            [whole(groups, LANE)] * 4 + [whole(entries, LANE)],
            2 * 4 * edges * entries * LANE,
            entries * LANE * 2 + 4 * edges * LANE * 2,
        )(own_slot, left_slot, right_slot, far_slot, arrived.reshape(entries, LANE))
    with jax.named_scope("send_senders"):
        got = lax.all_to_all(chosen, "edge", split_axis=0, concat_axis=0, tiled=True)
    with jax.named_scope("edge_update"):
        args, specs = zip(*[weights(k) for k in (W_SEND, W_OUT, W_AGG)])
        edge_out, term = call(
            edge_kernel,
            (weight((edges, width), BF16), weight((4, nodes, hid), BF16)),
            [
                whole(edges, width), whole(edges, hid), whole(4, LANE, groups * LANE),
                whole(groups, LANE), whole(nodes, width), whole(part, hid), whole(1, width),
            ]
            + sum(specs, []),
            2 * (2 * edges + 2 * nodes) * width * hid,
            edges * width * 10 + 3 * width * hid * 2,
            scratch=[
                pltpu.VMEM((edges, hid), BF16),
                pltpu.VMEM((edges, width), BF16),
                pltpu.VMEM((nodes, width), BF16),
            ],
        )(
            edge_feat, base, got, recv, node_feat, node_w_self, edge_gain.reshape(1, width),
            *sum(args, ()),
        )
    with jax.named_scope("send_terms"):
        terms = lax.all_to_all(term, "edge", split_axis=0, concat_axis=0, tiled=True)
    with jax.named_scope("node_update"):
        args, specs = weights(W_NODE)
        node_out = call(
            node_kernel,
            weight((nodes, width), BF16),
            [whole(4, nodes, hid), whole(nodes, width), whole(1, width)] + specs,
            2 * nodes * width * hid,
            nodes * width * 12 + width * hid * 2,
            scratch=[pltpu.VMEM((nodes, hid), BF16)],
        )(terms, node_feat, node_gain.reshape(1, width), *args)
    return (node_out, edge_out)


def solution(mesh):
    in_specs = (
        P("dom", None),
        P(("dom", "edge"), None),
        P(("dom", "edge")),
        P(("dom", "edge")),
        P("dom", None, None),
        P("edge", None),
        P("edge", None),
        P("edge", None),
        P("edge", None),
        P(),
        P("edge", None),
        P("edge", None),
        P("edge", None),
        P(),
    )
    out_specs = (P("dom", None), P(("dom", "edge"), None))
    return jax.shard_map(local, mesh=mesh, in_specs=in_specs, out_specs=out_specs, check_vma=False)
```

time: 194 us -> 102 us (0.53)
  blocking collectives: 66.7 us -> 15.6 us
  waiting for transfers between devices: 64.2 us -> 17.5 us
  starting transfers between devices: 17.6 us -> 43.4 us
  between operations: 14.3 us -> 0.87 us
  Pallas kernels: 0 us -> 12 us
  matrix products: 8.98 us -> 0 us
  local copies, waits for them, and re-layouts: 15.7 us -> 10.2 us
  other arithmetic: 5.57 us -> 1.23 us
    all_gather x5 -> x0, blocking collectives: 66.7 us -> none  [the longest x1 14.1 us: local(): lax.all_gather(edge_w_send, 'edge', axis=0, tiled=True)]
    psum x1 -> x0, waiting for transfers between devices: 52.1 us -> none  [local(): lax.psum(partial_pre.astype(jnp.bfloat16), 'edge').astype(jnp.float32)]
    ppermute x0 -> x7, starting transfers between devices: none -> 21.5 us  [the longest x1 4.21 us: local(): far_half = lax.ppermute(own_half, 'edge', ring(2))]
    all_to_all x0 -> x1, blocking collectives: none -> 15.6 us  [local(): lax.all_to_all(term, 'edge', split_axis=0, concat_axis=0, tiled=True)]
    ppermute x0 -> x7, waiting for transfers between devices: none -> 12.7 us  [the longest x1 8.52 us: local(): far_half = lax.ppermute(own_half, 'edge', ring(2))]
    unnamed x3 -> x0, waiting for transfers between devices: 12.1 us -> none
    pallas_call x0 -> x6, Pallas kernels: none -> 12 us  [the longest x1 3.13 us: local(): call(edge_kernel, (weight((edges, width), BF16), weight((4, nodes, hid),...]
    gather x2 -> x0, local copies, waits for them, and re-layouts: 11.2 us -> none  [the longest x1 8.57 us: local(): jnp.take(node_feat, listed_rows, axis=0)]
  transfers between devices with their start and end apart: 3 -> 9, of which waited for: 2 -> 3; matrix products, arithmetic and copies ran while one was open for 2% -> 1% of each run, Pallas kernels for 0% -> 6%
where the time goes in v1:
time: 102 us; the launch traced here: 101 us
  starting transfers between devices  43.4 us (43%)
  waiting for transfers between devices  17.5 us (17%)
  blocking collectives  15.6 us (15%)
  Pallas kernels  12 us (12%)
  local copies, waits for them, and re-layouts  10.2 us (10%)
  other arithmetic  1.23 us (1%)
    all_to_all x1, starting transfers between devices, local(): lax.all_to_all(outgoing.reshape(peers, slots, LANE), 'dom', split_axis=0,...  17.8 us
    all_to_all x1, blocking collectives, local(): lax.all_to_all(term, 'edge', split_axis=0, concat_axis=0, tiled=True)  15.6 us
    unnamed x36, local copies, waits for them, and re-layouts  10.2 us
    ppermute x1, waiting for transfers between devices, local(): far_half = lax.ppermute(own_half, 'edge', ring(2))  8.52 us
    all_to_all x1, waiting for transfers between devices, local(): lax.all_to_all(chosen, 'edge', split_axis=0, concat_axis=0, tiled=True)  4.76 us
    ppermute x1, starting transfers between devices, local(): far_half = lax.ppermute(own_half, 'edge', ring(2))  4.21 us
    ppermute x1, starting transfers between devices, local(): far_slot = lax.ppermute(own_slot, 'edge', ring(2))  4.21 us
    ppermute x1, waiting for transfers between devices, local(): left_slot = lax.ppermute(own_slot, 'edge', ring(1))  4.16 us
  transfers between devices with their start and end apart: 9, of which 3 were waited for; matrix products, arithmetic and copies ran while one was open for 1% of the time, Pallas kernels for 6%

profile of v1, /device:TPU:56, one launch (start us, length us, event | category | flops | bytes accessed | tf_op | source)
XLA Modules:
  0.0 100.8 jit_solution(15157216816625431153)
XLA Ops:
  0.6 0.0 copy-start.2
  0.6 0.0 copy-start.7
  0.7 0.9 copy-done.7
  1.6 0.9 copy-done.8
  2.5 0.9 copy-done.9
  3.4 0.9 copy-done.10
  4.3 0.9 copy-done.11
  5.2 0.9 copy-done.12
  6.1 1.6 %pack_shards.1 = (bf16[6,128,512]{2,1,0:T(8,128)(2,1)S(1)}, bf16[3,128,512]{2,1,0:T(8,128)(2,1)S(1)}) custom-call(bf16[128,512]{1,0:T(8,128)(2,1)S(1)} %copy-done.7, bf16[128,512]{1,0:T(8,128)(2,1)S(1)} %copy-done.8, bf16[128,512]{1,0:T(8,128)(2,1)S(1)} %copy-done.9, bf16[128,512]{1,0:T(8,128)(2,1)S(1)} %copy-done.10, bf16[128,512]{1,0:T(8,128)(2,1)S(1)} %copy-done.11, ...), custom_call_target="tpu_custom_call" | custom-call | bytes 2359296 | tf_op jit(solution)/shard_map/pack_shards/pallas_call | solution.py:250
  7.7 3.4 %collective-permute-start = (bf16[6,128,512]{2,1,0:T(8,128)(2,1)S(1)}, bf16[6,128,512]{2,1,0:T(8,128)(2,1)S(1)}, u32[]{:S(2)}, u32[]{:S(2)}) collective-permute-start(bf16[6,128,512]{2,1,0:T(8,128)(2,1)S(1)} %get-tuple-element.6.e0.r0.s0.o0.a0.n0), channel_id=1, source_target_pairs={{0,1},{1,2},{2,3},{3,0},{4,7},{5,4},{6,5},{7,6},{8,9},{9,10},{10,1... | collective-permute-start | bytes 2359304 | tf_op jit(solution)/shard_map/send_shards/ppermute | solution.py:260
  11.1 0.0 copy-done.2
  11.1 0.0 copy-done.17
  11.1 2.1 %pick_listed.1 = bf16[2048,128]{1,0:T(8,128)(2,1)} custom-call(s32[16,128]{1,0:T(8,128)S(1)} %bitcast.19, bf16[256,512]{1,0:T(8,128)(2,1)S(1)} %copy-done.2), custom_call_target="tpu_custom_call" | custom-call | flops 335544320 | bytes 786432 | tf_op jit(solution)/shard_map/pick_listed/pallas_call | solution.py:237
  13.2 17.8 %all-to-all-start = ((bf16[128,16,128]{2,1,0:T(8,128)(2,1)}), bf16[128,16,128]{2,1,0:T(8,128)(2,1)S(1)}, u32[]{:S(2)}, u32[]{:S(2)}) async-start(bf16[128,16,128]{2,1,0:T(8,128)(2,1)} %bitcast.4), calls=%async_computation | async-start | bytes 1048576 | tf_op jit(solution)/shard_map/send_listed/all_to_all | solution.py:245
  31.0 0.0 copy-start.14
  31.0 4.2 %collective-permute-start.2 = (bf16[3,128,512]{2,1,0:T(8,128)(2,1)S(1)}, bf16[3,128,512]{2,1,0:T(8,128)(2,1)}, u32[]{:S(2)}, u32[]{:S(2)}) collective-permute-start(bf16[3,128,512]{2,1,0:T(8,128)(2,1)S(1)} %get-tuple-element.7), channel_id=1, source_target_pairs={{0,2},{1,3},{2,0},{3,1},{4,6},{5,7},{6,4},{7,5},{8,10},{9,11},{10,... | collective-permute-start | bytes 1179656 | tf_op jit(solution)/shard_map/send_shards/ppermute | solution.py:261
  35.2 0.0 collective-permute-done.e1.r1.s1.o1.a1.n1
  35.2 1.9 %collective-permute-start.1 = (bf16[6,128,512]{2,1,0:T(8,128)(2,1)S(1)}, bf16[6,128,512]{2,1,0:T(8,128)(2,1)S(1)}, u32[]{:S(2)}, u32[]{:S(2)}) collective-permute-start(bf16[6,128,512]{2,1,0:T(8,128)(2,1)S(1)} %collective-permute-done.e1.r1.s1.o1.a1.n1), channel_id=1, source_target_pairs={{0,4},{4,0},{8,12},{12,8},{16,20},{20,16},{24,28},{28,24},{32,36},... | collective-permute-start | bytes 2359304 | tf_op jit(solution)/shard_map/send_shards/ppermute | solution.py:262
  37.1 8.5 %collective-permute-done.2 = bf16[3,128,512]{2,1,0:T(8,128)(2,1)} collective-permute-done((bf16[3,128,512]{2,1,0:T(8,128)(2,1)S(1)}, bf16[3,128,512]{2,1,0:T(8,128)(2,1)}, u32[]{:S(2)}, u32[]{:S(2)}) %collective-permute-start.2) | collective-permute-done | bytes 393248 | tf_op jit(solution)/shard_map/send_shards/ppermute | solution.py:261
  45.7 1.9 %collective-permute-start.3 = (bf16[3,128,512]{2,1,0:T(8,128)(2,1)}, bf16[3,128,512]{2,1,0:T(8,128)(2,1)}, u32[]{:S(2)}, u32[]{:S(2)}) collective-permute-start(bf16[3,128,512]{2,1,0:T(8,128)(2,1)} %collective-permute-done.2), channel_id=1, source_target_pairs={{0,4},{4,0},{8,12},{12,8},{16,20},{20,16},{24,28},{28,24},{32,36},... | collective-permute-start | bytes 1179656 | tf_op jit(solution)/shard_map/send_shards/ppermute | solution.py:263
  47.6 4.2 %collective-permute-start.6 = (s32[4,128]{1,0:T(4,128)S(1)}, s32[4,128]{1,0:T(4,128)S(1)}, u32[]{:S(2)}, u32[]{:S(2)}) collective-permute-start(s32[4,128]{1,0:T(4,128)S(1)} %bitcast.12), channel_id=1, source_target_pairs={{0,2},{1,3},{2,0},{3,1},{4,6},{5,7},{6,4},{7,5},{8,10},{9,11},{10,... | collective-permute-start | bytes 6152 | tf_op jit(solution)/shard_map/send_slots/ppermute | solution.py:270
  51.8 3.3 %collective-permute-start.5 = (s32[4,128]{1,0:T(4,128)S(1)}, s32[4,128]{1,0:T(4,128)S(1)}, u32[]{:S(2)}, u32[]{:S(2)}) collective-permute-start(s32[4,128]{1,0:T(4,128)S(1)} %bitcast.13), channel_id=1, source_target_pairs={{0,3},{1,0},{2,1},{3,2},{4,7},{5,4},{6,5},{7,6},{8,11},{9,8},{10,9... | collective-permute-start | bytes 6152 | tf_op jit(solution)/shard_map/send_slots/ppermute | solution.py:269
  55.2 2.5 %collective-permute-start.4 = (s32[4,128]{1,0:T(4,128)S(1)}, s32[4,128]{1,0:T(4,128)S(1)}, u32[]{:S(2)}, u32[]{:S(2)}) collective-permute-start(s32[4,128]{1,0:T(4,128)S(1)} %bitcast.14), channel_id=1, source_target_pairs={{0,1},{1,2},{2,3},{3,0},{4,5},{5,6},{6,7},{7,4},{8,9},{9,10},{10,1... | collective-permute-start | bytes 6152 | tf_op jit(solution)/shard_map/send_slots/ppermute | solution.py:268
  57.7 0.0 collective-permute-done.6.far_ref
  57.7 0.0 collective-permute-done.5.right_ref
  57.7 4.2 %collective-permute-done.4.left_ref = s32[4,128]{1,0:T(4,128)S(1)} collective-permute-done((s32[4,128]{1,0:T(4,128)S(1)}, s32[4,128]{1,0:T(4,128)S(1)}, u32[]{:S(2)}, u32[]{:S(2)}) %collective-permute-start.4) | collective-permute-done | bytes 2080 | tf_op jit(solution)/shard_map/send_slots/ppermute | solution.py:268
  61.8 0.0 all-to-all-done
  61.8 2.8 %choose_senders.1 = bf16[4,128,512]{2,1,0:T(8,128)(2,1)S(1)} custom-call(s32[4,128]{1,0:T(4,128)S(1)} %bitcast.15, s32[4,128]{1,0:T(4,128)S(1)} %collective-permute-done.4.left_ref, s32[4,128]{1,0:T(4,128)S(1)} %collective-permute-done.5.right_ref, s32[4,128]{1,0:T(4,128)S(1)} %collective-permute-done.6.far_ref, bf16[2048,128]{1,0:T(8,128)(2,1)S(1)} %bitcast.9), custom_call_target="tpu_custom_call" | custom-call | flops 1073741824 | bytes 1048576 | tf_op jit(solution)/shard_map/choose_senders/pallas_call | solution.py:290
  64.7 0.0 copy-start.5
  64.7 0.8 copy-done.5
  65.5 4.1 %all-to-all-start.1 = ((bf16[4,128,512]{2,1,0:T(8,128)(2,1)}), bf16[4,128,512]{2,1,0:T(8,128)(2,1)}, u32[]{:S(2)}, u32[]{:S(2)}) async-start(bf16[4,128,512]{2,1,0:T(8,128)(2,1)} %copy-done.5), calls=%async_computation.1 | async-start | bytes 1048576 | tf_op jit(solution)/shard_map/send_senders/all_to_all | solution.py:298
  69.6 0.0 copy-start.3
  69.6 0.0 collective-permute-done.3
  69.6 1.2 %broadcast_select_fusion = (bf16[3,128,512]{2,1,0:T(8,128)(2,1)S(1)}, bf16[3,128,512]{2,1,0:T(8,128)(2,1)S(1)}) fusion(bf16[3,128,512]{2,1,0:T(8,128)(2,1)} %collective-permute-done.3, bf16[3,128,512]{2,1,0:T(8,128)(2,1)} %collective-permute-done.2, pred[]{:T(512)S(6)} %eq.4), kind=kLoop, calls=%fused_computation | loop fusion | flops 393216 | bytes 1572865 | tf_op jit(solution)/shard_map/send_shards/select_n | solution.py:265
  70.9 0.0 copy-start.13
  70.9 0.0 collective-permute-done.1.e2.r2.s2.o2.a2.n2
  70.9 0.0 copy-done.3
  70.9 0.7 copy-done.13
  71.6 1.1 %edge_pre_local.1.base_ref = f32[512,512]{1,0:T(8,128)S(1)} custom-call(bf16[512,512]{1,0:T(8,128)(2,1)S(1)} %copy-done.3, bf16[256,512]{1,0:T(8,128)(2,1)S(1)} %copy-done.2, s32[4,128]{1,0:T(4,128)S(1)} %bitcast.16, s32[4,128]{1,0:T(4,128)S(1)} %bitcast.10, bf16[6,128,512]{2,1,0:T(8,128)(2,1)S(1)} %get-tuple-element.6.e0.r0.s0.o0.a0.n0, ...), custom_call_target="tpu_custom_call" | custom-call | flops 805306368 | bytes 3145728 | tf_op jit(solution)/shard_map/edge_pre_local/pallas_call | solution.py:280
  72.6 0.0 copy-start
  72.6 1.0 copy-done
  73.6 4.8 %all-to-all-done.1.got_ref = bf16[4,128,512]{2,1,0:T(8,128)(2,1)} async-done(((bf16[4,128,512]{2,1,0:T(8,128)(2,1)}), bf16[4,128,512]{2,1,0:T(8,128)(2,1)}, u32[]{:S(2)}, u32[]{:S(2)}) %all-to-all-start.1) | async-done | bytes 524320 | tf_op jit(solution)/shard_map/send_senders/all_to_all | solution.py:298
  78.4 1.2 %copy-done.1 = f32[512,512]{1,0:T(8,128)S(1)} copy-done((f32[512,512]{1,0:T(8,128)S(1)}, f32[512,512]{1,0:T(8,128)}, u32[]{:S(2)}) %copy-start.1) | copy-done | bytes 1048600
  79.6 1.0 %copy-done.4 = bf16[512,512]{1,0:T(8,128)(2,1)S(1)} copy-done((bf16[512,512]{1,0:T(8,128)(2,1)S(1)}, bf16[512,512]{1,0:T(8,128)(2,1)}, u32[]{:S(2)}) %copy-start.4) | copy-done | bytes 524312
  80.6 3.1 %edge_update.1 = (bf16[512,512]{1,0:T(8,128)(2,1)}, bf16[4,256,512]{2,1,0:T(8,128)(2,1)S(1)}) custom-call(bf16[512,512]{1,0:T(8,128)(2,1)S(1)} %copy-done.4, f32[512,512]{1,0:T(8,128)S(1)} %copy-done.1, bf16[4,128,512]{2,1,0:T(8,128)(2,1)} %all-to-all-done.1.got_ref, s32[4,128]{1,0:T(4,128)S(1)} %bitcast.11, bf16[256,512]{1,0:T(8,128)(2,1)S(1)} %copy-done.2, ...), custom_call_target="tpu_custom_call" | custom-call | flops 805306368 | bytes 4194304 | tf_op jit(solution)/shard_map/edge_update/pallas_call | solution.py:301
  83.8 15.6 %all_to_all.15.terms_ref = bf16[4,256,512]{2,1,0:T(8,128)(2,1)S(1)} all-to-all(bf16[4,256,512]{2,1,0:T(8,128)(2,1)S(1)} %get-tuple-element.8), channel_id=1, replica_groups=mesh['dom'=128,'edge'=4] {'edge'}, dimensions={0} | all-to-all | bytes 2097152 | tf_op jit(solution)/shard_map/send_terms/all_to_all | solution.py:321
  99.4 0.0 copy-done.16
  99.4 1.4 %node_update.1 = bf16[256,512]{1,0:T(8,128)(2,1)} custom-call(bf16[4,256,512]{2,1,0:T(8,128)(2,1)S(1)} %all_to_all.15.terms_ref, bf16[256,512]{1,0:T(8,128)(2,1)S(1)} %copy-done.2, f32[1,512]{1,0:T(1,128)S(1)} %bitcast.18, bf16[6,128,512]{2,1,0:T(8,128)(2,1)S(1)} %get-tuple-element.6.e0.r0.s0.o0.a0.n0, ...), custom_call_target="tpu_custom_call" | custom-call | flops 134217728 | bytes 2097152 | tf_op jit(solution)/shard_map/node_update/pallas_call | solution.py:324
  (14 shorter events, 0.0 us)
Async XLA Ops:
  0.6 10.5 %copy-start.2 = (bf16[256,512]{1,0:T(8,128)(2,1)S(1)}, bf16[256,512]{1,0:T(8,128)(2,1)}, u32[]{:S(2)}) copy-start(bf16[256,512]{1,0:T(8,128)(2,1)} %node_ref.7) | copy-start | bytes 786436
  0.6 0.9 copy-start.7
  1.6 0.9 copy-start.8
  2.5 0.9 copy-start.9
  3.4 0.9 copy-start.10
  4.3 0.9 copy-start.11
  5.2 0.9 copy-start.12
  6.1 5.0 %copy-start.17 = (s32[1,128,16]{1,2,0:T(8,128)S(1)}, s32[1,128,16]{1,2,0:T(8,128)}, u32[]{:S(2)}) copy-start(s32[1,128,16]{1,2,0:T(8,128)} %param.18) | copy-start | bytes 24580
  7.7 27.5 %collective-permute-start = (bf16[6,128,512]{2,1,0:T(8,128)(2,1)S(1)}, bf16[6,128,512]{2,1,0:T(8,128)(2,1)S(1)}, u32[]{:S(2)}, u32[]{:S(2)}) collective-permute-start(bf16[6,128,512]{2,1,0:T(8,128)(2,1)S(1)} %get-tuple-element.6.e0.r0.s0.o0.a0.n0), channel_id=1, source_target_pairs={{0,1},{1,2},{2,3},{3,0},{4,7},{5,4},{6,5},{7,6},{8,9},{9,10},{10,1... | collective-permute-start | bytes 2359304 | tf_op jit(solution)/shard_map/send_shards/ppermute | solution.py:260
  13.2 48.6 %all-to-all-start = ((bf16[128,16,128]{2,1,0:T(8,128)(2,1)}), bf16[128,16,128]{2,1,0:T(8,128)(2,1)S(1)}, u32[]{:S(2)}, u32[]{:S(2)}) async-start(bf16[128,16,128]{2,1,0:T(8,128)(2,1)} %bitcast.4), calls=%async_computation | async-start | bytes 1048576 | tf_op jit(solution)/shard_map/send_listed/all_to_all | solution.py:245
  31.0 16.6 %copy-start.14 = (s32[512]{0:T(512)S(1)}, s32[512]{0:T(512)}, u32[]{:S(2)}) copy-start(s32[512]{0:T(512)} %param.16) | copy-start | bytes 6148
  31.0 14.7 %collective-permute-start.2 = (bf16[3,128,512]{2,1,0:T(8,128)(2,1)S(1)}, bf16[3,128,512]{2,1,0:T(8,128)(2,1)}, u32[]{:S(2)}, u32[]{:S(2)}) collective-permute-start(bf16[3,128,512]{2,1,0:T(8,128)(2,1)S(1)} %get-tuple-element.7), channel_id=1, source_target_pairs={{0,2},{1,3},{2,0},{3,1},{4,6},{5,7},{6,4},{7,5},{8,10},{9,11},{10,... | collective-permute-start | bytes 1179656 | tf_op jit(solution)/shard_map/send_shards/ppermute | solution.py:261
  35.2 35.7 %collective-permute-start.1 = (bf16[6,128,512]{2,1,0:T(8,128)(2,1)S(1)}, bf16[6,128,512]{2,1,0:T(8,128)(2,1)S(1)}, u32[]{:S(2)}, u32[]{:S(2)}) collective-permute-start(bf16[6,128,512]{2,1,0:T(8,128)(2,1)S(1)} %collective-permute-done.e1.r1.s1.o1.a1.n1), channel_id=1, source_target_pairs={{0,4},{4,0},{8,12},{12,8},{16,20},{20,16},{24,28},{28,24},{32,36},... | collective-permute-start | bytes 2359304 | tf_op jit(solution)/shard_map/send_shards/ppermute | solution.py:262
  45.7 24.0 %collective-permute-start.3 = (bf16[3,128,512]{2,1,0:T(8,128)(2,1)}, bf16[3,128,512]{2,1,0:T(8,128)(2,1)}, u32[]{:S(2)}, u32[]{:S(2)}) collective-permute-start(bf16[3,128,512]{2,1,0:T(8,128)(2,1)} %collective-permute-done.2), channel_id=1, source_target_pairs={{0,4},{4,0},{8,12},{12,8},{16,20},{20,16},{24,28},{28,24},{32,36},... | collective-permute-start | bytes 1179656 | tf_op jit(solution)/shard_map/send_shards/ppermute | solution.py:263
  47.6 10.1 %collective-permute-start.6 = (s32[4,128]{1,0:T(4,128)S(1)}, s32[4,128]{1,0:T(4,128)S(1)}, u32[]{:S(2)}, u32[]{:S(2)}) collective-permute-start(s32[4,128]{1,0:T(4,128)S(1)} %bitcast.12), channel_id=1, source_target_pairs={{0,2},{1,3},{2,0},{3,1},{4,6},{5,7},{6,4},{7,5},{8,10},{9,11},{10,... | collective-permute-start | bytes 6152 | tf_op jit(solution)/shard_map/send_slots/ppermute | solution.py:270
  51.8 5.9 %collective-permute-start.5 = (s32[4,128]{1,0:T(4,128)S(1)}, s32[4,128]{1,0:T(4,128)S(1)}, u32[]{:S(2)}, u32[]{:S(2)}) collective-permute-start(s32[4,128]{1,0:T(4,128)S(1)} %bitcast.13), channel_id=1, source_target_pairs={{0,3},{1,0},{2,1},{3,2},{4,7},{5,4},{6,5},{7,6},{8,11},{9,8},{10,9... | collective-permute-start | bytes 6152 | tf_op jit(solution)/shard_map/send_slots/ppermute | solution.py:269
  55.2 6.7 %collective-permute-start.4 = (s32[4,128]{1,0:T(4,128)S(1)}, s32[4,128]{1,0:T(4,128)S(1)}, u32[]{:S(2)}, u32[]{:S(2)}) collective-permute-start(s32[4,128]{1,0:T(4,128)S(1)} %bitcast.14), channel_id=1, source_target_pairs={{0,1},{1,2},{2,3},{3,0},{4,5},{5,6},{6,7},{7,4},{8,9},{9,10},{10,1... | collective-permute-start | bytes 6152 | tf_op jit(solution)/shard_map/send_slots/ppermute | solution.py:268
  64.7 0.8 copy-start.5
  65.5 12.9 %all-to-all-start.1 = ((bf16[4,128,512]{2,1,0:T(8,128)(2,1)}), bf16[4,128,512]{2,1,0:T(8,128)(2,1)}, u32[]{:S(2)}, u32[]{:S(2)}) async-start(bf16[4,128,512]{2,1,0:T(8,128)(2,1)} %copy-done.5), calls=%async_computation.1 | async-start | bytes 1048576 | tf_op jit(solution)/shard_map/send_senders/all_to_all | solution.py:298
  69.6 1.3 %copy-start.3 = (bf16[512,512]{1,0:T(8,128)(2,1)S(1)}, bf16[512,512]{1,0:T(8,128)(2,1)}, u32[]{:S(2)}) copy-start(bf16[512,512]{1,0:T(8,128)(2,1)} %edge_ref.3) | copy-start | bytes 1572868
  70.9 0.7 copy-start.13
  71.6 6.8 %copy-start.6 = (bf16[128,512]{1,0:T(8,128)(2,1)S(1)}, bf16[128,512]{1,0:T(8,128)(2,1)}, u32[]{:S(2)}) copy-start(bf16[128,512]{1,0:T(8,128)(2,1)} %self_ref.1) | copy-start | bytes 393220
  72.6 1.0 copy-start
  73.6 4.8 %copy-start.15 = (f32[512]{0:T(512)S(1)}, f32[512]{0:T(512)}, u32[]{:S(2)}) copy-start(f32[512]{0:T(512)} %param.23) | copy-start | bytes 6148
  78.4 1.2 %copy-start.1 = (f32[512,512]{1,0:T(8,128)S(1)}, f32[512,512]{1,0:T(8,128)}, u32[]{:S(2)}) copy-start(f32[512,512]{1,0:T(8,128)} %copy-done) | copy-start | bytes 3145732
  79.6 1.0 %copy-start.4 = (bf16[512,512]{1,0:T(8,128)(2,1)S(1)}, bf16[512,512]{1,0:T(8,128)(2,1)}, u32[]{:S(2)}) copy-start(bf16[512,512]{1,0:T(8,128)(2,1)} %edge_ref.3) | copy-start | bytes 1572868
  83.8 15.6 %copy-start.16 = (f32[512]{0:T(512)S(1)}, f32[512]{0:T(512)}, u32[]{:S(2)}) copy-start(f32[512]{0:T(512)} %param.27) | copy-start | bytes 6148

commit v2 on v1

v2 whole, which is shorter than its diff:
```python
import functools

import jax
import jax.numpy as jnp
from jax import lax
from jax.experimental import pallas as pl
from jax.experimental.pallas import tpu as pltpu
from jax.sharding import PartitionSpec as P

F32 = jnp.float32
BF16 = jnp.bfloat16
LANE = 128
VMEM_BYTES = 24 * 1024 * 1024

W_NODE, W_EDGE, W_RECV, W_SEND, W_OUT, W_AGG = range(6)
HALF = 3
NOTE = 16


def whole(*shape):
    return pl.BlockSpec(shape, lambda i: (0,) * len(shape))


def block_of(index, *shape):
    return pl.BlockSpec(shape, lambda i: (index,) + (0,) * (len(shape) - 1))


def in_hbm(*arrays):
    return [pltpu.with_memory_space_constraint(a, pltpu.HBM) for a in arrays]


def call(body, outs, in_specs, flops, nbytes, scratch=(), out_specs=None):
    return pl.pallas_call(
        body,
        out_shape=outs,
        grid=(1,),
        in_specs=in_specs,
        out_specs=out_specs
        if out_specs is not None
        else jax.tree.map(lambda o: whole(*o.shape), outs),
        scratch_shapes=scratch,
        compiler_params=pltpu.CompilerParams(vmem_limit_bytes=VMEM_BYTES),
        cost_estimate=pl.CostEstimate(flops=flops, bytes_accessed=nbytes, transcendentals=0),
    )


def silu(v):
    return 0.5 * v * (1.0 + jnp.tanh(0.5 * v))


def normalize(v):
    center = v - jnp.mean(v, axis=-1, keepdims=True)
    spread = jnp.mean(center * center, axis=-1, keepdims=True)
    return center * lax.rsqrt(spread + 1e-05)


def dot(a, b):
    return jnp.dot(a, b, preferred_element_type=F32)


def shard_order():
    x = lax.axis_index("edge")
    core = lax.rem(lax.axis_index("dom"), 2)
    step = jnp.where(core == 0, 3, 1)
    return (x, lax.rem(x + step, 4), lax.rem(x + 4 - step, 4), lax.rem(x + 2, 4))


def columns(j):
    return pl.ds(pl.multiple_of(j * LANE, LANE), LANE)


def by_shard(ref, rows, order):
    return jnp.concatenate([ref[rows, columns(j)] for j in order], axis=1)


def stacked(refs, place=0):
    return jnp.concatenate([r[place * LANE : (place + 1) * LANE, :] for r in refs], axis=0)


def column_of(row_block):
    return jnp.transpose(row_block.astype(F32))


def pick_kernel(listed_hbm, node_hbm, slot_hbm, *refs):
    shards = refs[:6]
    out_ref, packed, listed_ref, node_ref, slot_ref, note_ref, sem = refs[6:]
    part = shards[0].shape[0]
    mine = columns(lax.axis_index("edge"))
    first = [
        pltpu.make_async_copy(listed_hbm, listed_ref, sem.at[0]),
        pltpu.make_async_copy(node_hbm.at[:, mine], node_ref, sem.at[1]),
        pltpu.make_async_copy(slot_hbm, slot_ref, sem.at[2]),
    ]
    copies = []
    for k, shard in enumerate(shards):
        at = k * part + (NOTE if k >= HALF else 0)
        copies.append(pltpu.make_async_copy(shard, packed.at[at : at + part, :], sem.at[3 + k]))
    for c in first + copies:
        c.start()
    first[2].wait()
    groups = slot_ref.shape[0]
    note_ref[...] = jnp.zeros_like(note_ref)
    high = lax.shift_right_logical(slot_ref[...], 4)
    low = jnp.bitwise_and(slot_ref[...], 15)
    note_ref[0:NOTE, 0 : 2 * LANE] = jnp.concatenate(
        [
            jnp.concatenate([v.astype(F32), jnp.zeros((NOTE - groups, LANE), F32)], axis=0)
            for v in (high, low)
        ],
        axis=1,
    ).astype(BF16)
    for k, at in enumerate((HALF * part, 2 * HALF * part + NOTE)):
        copies.append(
            pltpu.make_async_copy(note_ref, packed.at[at : at + NOTE, :], sem.at[9 + k])
        )
        copies[-1].start()
    slots, peers = listed_ref.shape
    nodes = node_ref.shape[0]
    first[0].wait()
    listed = listed_ref[...].astype(F32).astype(BF16)
    first[1].wait()
    mine = node_ref[...]
    rows = min(512, peers * slots)
    shift = slots.bit_length() - 1
    ones = jnp.ones((slots, nodes), BF16)
    for base in range(0, peers * slots, rows):
        place = base + lax.broadcasted_iota(jnp.int32, (rows, peers), 0)
        peer = lax.broadcasted_iota(jnp.int32, (rows, peers), 1)
        spread = jnp.where(lax.shift_right_logical(place, shift) == peer, 1.0, 0.0).astype(BF16)
        found = lax.dot_general(
            spread, listed, (((1,), (1,)), ((), ())), preferred_element_type=F32
        )
        slot = jnp.bitwise_and(lax.broadcasted_iota(jnp.int32, (rows, slots), 0), slots - 1)
        lane = lax.broadcasted_iota(jnp.int32, (rows, slots), 1)
        found = jnp.where(slot == lane, found, 0.0).astype(BF16)
        wanted = dot(found, ones)
        node = lax.broadcasted_iota(jnp.int32, (rows, nodes), 1).astype(F32)
        onehot = jnp.where(wanted == node, 1.0, 0.0).astype(BF16)
        out_ref[base : base + rows, :] = dot(onehot, mine).astype(BF16)
    for c in copies:
        c.wait()


def noted(block, groups):
    v = block[:, 0 : 2 * LANE].astype(F32)
    return (v[:groups, :LANE] * 16.0 + v[:groups, LANE:]).astype(jnp.int32)


def choose_kernel(
    nodes, own_ref, across_ref, near_ref, low_ref, high_ref, table_ref, out_ref, block_ref, sem
):
    order = shard_order()
    groups = own_ref.shape[0]
    core = lax.rem(lax.axis_index("dom"), 2)
    far = jnp.where(core == 0, high_ref[...].astype(F32), low_ref[...].astype(F32))
    all_slots = (
        own_ref[...],
        noted(near_ref[...], groups),
        across_ref[...],
        noted(far, groups),
    )
    entries = table_ref.shape[0]
    width = 256
    lane = lax.broadcasted_iota(jnp.int32, (LANE, width), 1).astype(F32)
    copies = []
    for k, slots in enumerate(all_slots):
        wanted = column_of(slots - nodes)
        for g in range(groups):
            total = jnp.zeros((LANE, LANE), F32)
            for base in range(0, entries, width):
                w = min(width, entries - base)
                onehot = jnp.where(
                    wanted[:, g : g + 1] - float(base) == lane[:, :w], 1.0, 0.0
                ).astype(BF16)
                total = total + dot(onehot, table_ref[base : base + w, :])
            block_ref[k, :, g * LANE : (g + 1) * LANE] = total.astype(BF16)
        copies.append(pltpu.make_async_copy(block_ref.at[k], out_ref.at[order[k]], sem.at[k]))
        copies[-1].start()
    for c in copies:
        c.wait()


def base_kernel(
    edge_ref, node_ref, slot_ref, recv_ref,
    e0, e1, e2, e3, r0, r1, r2, r3, h0, h1, h2, h3, out_ref, table_ref, base_ref, sem,
):
    order = shard_order()
    nodes = node_ref.shape[0]
    by_node = by_shard(node_ref, slice(None), order)
    table_ref[0] = dot(by_node, stacked((h0, h1, h2, h3))).astype(BF16)
    table_ref[1] = dot(by_node, stacked((r0, r1, r2, r3))).astype(BF16)
    w_edge = stacked((e0, e1, e2, e3))
    slot = column_of(slot_ref[...])
    recv = column_of(recv_ref[...])
    lane = lax.broadcasted_iota(jnp.int32, (LANE, nodes), 1).astype(F32)
    copies = []
    for g in range(slot_ref.shape[0]):
        rows = slice(g * LANE, (g + 1) * LANE)
        from_slot = jnp.where(slot[:, g : g + 1] == lane, 1.0, 0.0).astype(BF16)
        from_recv = jnp.where(recv[:, g : g + 1] == lane, 1.0, 0.0).astype(BF16)
        total = dot(by_shard(edge_ref, rows, order), w_edge)
        total = total + dot(from_slot, table_ref[0])
        base_ref[rows, :] = total + dot(from_recv, table_ref[1])
        copies.append(pltpu.make_async_copy(base_ref.at[rows, :], out_ref.at[rows, :], sem.at[g]))
        copies[-1].start()
    for c in copies:
        c.wait()


def edge_kernel(
    edge_hbm, base_hbm, node_hbm, self_hbm, gain_hbm, got_ref, recv_ref, h0, h1, h2, h3,
    out_hbm, term_ref, edge_ref, base_ref, node_ref, self_ref, gain_ref, out_ref,
    hidden_ref, message_ref, total_ref, sem,
):
    order = shard_order()
    edges, width = edge_ref.shape
    mine = columns(lax.axis_index("edge"))
    blocks = [slice(g * LANE, (g + 1) * LANE) for g in range(edges // LANE)]
    base_in = [
        pltpu.make_async_copy(base_hbm.at[rows, :], base_ref.at[rows, :], sem.at[g])
        for g, rows in enumerate(blocks)
    ]
    later_in = [
        pltpu.make_async_copy(gain_hbm, gain_ref, sem.at[4]),
        pltpu.make_async_copy(edge_hbm, edge_ref, sem.at[5]),
        pltpu.make_async_copy(node_hbm.at[:, mine], node_ref, sem.at[6]),
        pltpu.make_async_copy(self_hbm, self_ref, sem.at[7]),
    ]
    for c in base_in + later_in:
        c.start()
    shards = (h0, h1, h2, h3)
    w_send = stacked(shards, 0)
    w_out = stacked(shards, 1)
    for g, rows in enumerate(blocks):
        sender = jnp.concatenate([got_ref[j, :, rows] for j in order], axis=1)
        before = dot(sender, w_send)
        base_in[g].wait()
        hidden_ref[rows, :] = silu(base_ref[rows, :] + before).astype(BF16)
    for c in later_in:
        c.wait()
    copies = []
    for g, rows in enumerate(blocks):
        message = normalize(dot(by_shard(hidden_ref, rows, order), w_out)) * gain_ref[...]
        out_ref[rows, :] = (edge_ref[rows, :].astype(F32) + message).astype(BF16)
        copies.append(pltpu.make_async_copy(out_ref.at[rows, :], out_hbm.at[rows, :], sem.at[8 + g]))
        copies[-1].start()
        message_ref[rows, :] = message.astype(BF16)
    node = lax.broadcasted_iota(jnp.int32, (node_ref.shape[0], LANE), 0)
    onehot = jnp.concatenate(
        [
            jnp.where(recv_ref[g : g + 1, :] == node, 1.0, 0.0).astype(BF16)
            for g in range(len(blocks))
        ],
        axis=1,
    )
    total_ref[...] = dot(onehot, message_ref[...]).astype(BF16)
    term = dot(by_shard(total_ref, slice(None), order), stacked(shards, 2))
    term = (term + dot(node_ref[...], self_ref[...])).astype(BF16)
    for j in range(term_ref.shape[0]):
        term_ref[j] = term
    for c in copies:
        c.wait()


def node_kernel(terms_ref, node_ref, gain_ref, n0, n1, n2, n3, out_ref, hidden_ref):
    order = shard_order()
    terms = [terms_ref[j].astype(F32) for j in range(terms_ref.shape[0])]
    hidden_ref[...] = silu((terms[0] + terms[1]) + (terms[2] + terms[3])).astype(BF16)
    update = normalize(
        dot(by_shard(hidden_ref, slice(None), order), stacked((n0, n1, n2, n3)))
    )
    out_ref[...] = (node_ref[...].astype(F32) + update * gain_ref[...]).astype(BF16)


def local(
    node_feat, edge_feat, edge_slot, edge_recv, send_list, edge_w_edge, edge_w_send, edge_w_recv,
    edge_w_out, edge_gain, node_w_self, node_w_agg, node_w_out, node_gain,
):
    peers = lax.axis_size("dom")
    core = lax.rem(lax.axis_index("dom"), 2)
    nodes, width = node_feat.shape
    edges = edge_feat.shape[0]
    part, hid = edge_w_edge.shape
    slots = send_list.shape[2]
    entries = peers * slots
    groups = edges // LANE
    weight = jax.ShapeDtypeStruct

    both = [
        (d * 4 + i, d * 4 + (i + (1 if d % 2 == 0 else 3)) % 4)
        for d in range(peers)
        for i in range(4)
    ]
    back = [(i, j) for j, i in both]
    swap = [(d, d ^ 1) for d in range(peers)]

    anywhere = pl.BlockSpec(memory_space=pltpu.HBM)
    dma = pltpu.SemaphoreType.DMA
    own_slot = edge_slot.reshape(groups, LANE)
    recv = edge_recv.reshape(groups, LANE)
    packed_rows = 2 * (HALF * part + NOTE)
    half_rows = HALF * part + NOTE

    with jax.named_scope("pick_listed"):
        outgoing, own_w = call(
            pick_kernel,
            (weight((entries, LANE), BF16), weight((packed_rows, hid), BF16)),
            [anywhere] * 9,
            2 * entries * 640 * LANE,
            entries * 256 + nodes * width * 2,
            scratch=[
                pltpu.VMEM((slots, peers), jnp.int32),
                pltpu.VMEM((nodes, LANE), BF16),
                pltpu.VMEM((groups, LANE), jnp.int32),
                pltpu.VMEM((NOTE, hid), BF16),
                dma((11,)),
            ],
            out_specs=(whole(entries, LANE), anywhere),
        )(
            *in_hbm(
                send_list[0].T, node_feat, own_slot,
                node_w_out, edge_w_edge, edge_w_recv, edge_w_send, edge_w_out, node_w_agg,
            )
        )
    with jax.named_scope("send_near"):
        near_w = lax.ppermute(own_w, ("dom", "edge"), both)
    with jax.named_scope("send_listed"):
        arrived = lax.all_to_all(
            outgoing.reshape(peers, slots, LANE), "dom", split_axis=0, concat_axis=0, tiled=True
        )
    with jax.named_scope("send_slots"):
        back_slot, _ = lax.optimization_barrier((own_slot, own_w))
        across_slot = lax.ppermute(back_slot, ("dom", "edge"), back)
    with jax.named_scope("send_far"):
        half = lax.dynamic_slice_in_dim(near_w, HALF * part * core, half_rows, 0)
        far_half = lax.ppermute(half, ("dom", "edge"), both)
    with jax.named_scope("swap_near"):
        across_w = lax.ppermute(near_w, "dom", swap)
    with jax.named_scope("swap_far"):
        across_half = lax.ppermute(far_half, "dom", swap)
        low_half = lax.select(core == 0, far_half[: half_rows - NOTE], across_half[: half_rows - NOTE])
        high_half = lax.select(core == 0, across_half[NOTE:], far_half[NOTE:])

    with jax.named_scope("choose_senders"):
        chosen = call(
            functools.partial(choose_kernel, nodes),
            weight((4, LANE, groups * LANE), BF16),
            [
                whole(groups, LANE), whole(groups, LANE),
                block_of(HALF * part // NOTE, NOTE, hid),
                block_of(0, NOTE, hid), block_of(HALF * part // NOTE, NOTE, hid),
                whole(entries, LANE),
            ],
            2 * 4 * edges * entries * LANE,
            entries * LANE * 2 + 4 * edges * LANE * 2,
            scratch=[pltpu.VMEM((4, LANE, groups * LANE), BF16), dma((4,))],
            out_specs=anywhere,
        )(
            own_slot, across_slot, near_w, far_half, far_half, arrived.reshape(entries, LANE),
        )
    with jax.named_scope("send_senders"):
        got = lax.all_to_all(chosen, "edge", split_axis=0, concat_axis=0, tiled=True)

    def low(k):
        return (own_w, near_w, across_w, low_half), [block_of(k, part, hid)] * 4

    high = (own_w, near_w, across_w, high_half)
    high_specs = [block_of(1, half_rows, hid)] * 3 + [whole(half_rows - NOTE, hid)]

    with jax.named_scope("edge_pre_local"):
        base = call(
            base_kernel,
            weight((edges, hid), F32),
            [whole(edges, width), whole(nodes, width), whole(groups, LANE), whole(groups, LANE)]
            + low(W_EDGE)[1] + low(W_RECV)[1] + high_specs,
            2 * (2 * edges + 2 * nodes) * width * hid,
            edges * width * 6 + 3 * width * hid * 2,
            scratch=[pltpu.VMEM((2, nodes, hid), BF16), pltpu.VMEM((edges, hid), F32), dma((groups,))],
            out_specs=anywhere,
        )(
            edge_feat, node_feat, own_slot, recv, *low(W_EDGE)[0], *low(W_RECV)[0], *high,
        )
    with jax.named_scope("edge_update"):
        edge_out, term = call(
            edge_kernel,
            (weight((edges, width), BF16), weight((4, nodes, hid), BF16)),
            [anywhere] * 5 + [whole(4, LANE, groups * LANE), whole(groups, LANE)] + high_specs,
            2 * (2 * edges + 2 * nodes) * width * hid,
            edges * width * 10 + 3 * width * hid * 2,
            scratch=[
                pltpu.VMEM((edges, width), BF16),
                pltpu.VMEM((edges, hid), F32),
                pltpu.VMEM((nodes, LANE), BF16),
                pltpu.VMEM((part, hid), BF16),
                pltpu.VMEM((1, width), F32),
                pltpu.VMEM((edges, width), BF16),
                pltpu.VMEM((edges, hid), BF16),
                pltpu.VMEM((edges, width), BF16),
                pltpu.VMEM((nodes, width), BF16),
                dma((12,)),
            ],
            out_specs=(anywhere, whole(4, nodes, hid)),
        )(
            *in_hbm(edge_feat, base, node_feat, node_w_self, edge_gain.reshape(1, width)),
            got, recv, *high,
        )
    with jax.named_scope("send_terms"):
        terms = lax.all_to_all(term, "edge", split_axis=0, concat_axis=0, tiled=True)
    with jax.named_scope("node_update"):
        args, specs = low(W_NODE)
        node_out = call(
            node_kernel,
            weight((nodes, width), BF16),
            [whole(4, nodes, hid), whole(nodes, width), whole(1, width)] + specs,
            2 * nodes * width * hid,
            nodes * width * 12 + width * hid * 2,
            scratch=[pltpu.VMEM((nodes, hid), BF16)],
        )(terms, node_feat, node_gain.reshape(1, width), *args)
    return (node_out, edge_out)


def solution(mesh):
    in_specs = (
        P("dom", None),
        P(("dom", "edge"), None),
        P(("dom", "edge")),
        P(("dom", "edge")),
        P("dom", None, None),
        P("edge", None),
        P("edge", None),
        P("edge", None),
        P("edge", None),
        P(),
        P("edge", None),
        P("edge", None),
        P("edge", None),
        P(),
    )
    out_specs = (P("dom", None), P(("dom", "edge"), None))
    return jax.shard_map(local, mesh=mesh, in_specs=in_specs, out_specs=out_specs, check_vma=False)
```

time: 102 us -> 87.3 us (0.86)
  starting transfers between devices: 43.4 us -> 34.7 us
  local copies, waits for them, and re-layouts: 10.2 us -> 2.52 us
  waiting for transfers between devices: 17.5 us -> 14.5 us
  Pallas kernels: 12 us -> 14.8 us
  blocking collectives: 15.6 us -> 17.9 us
    ppermute x4 -> x2, starting transfers between devices: 14.3 us -> 5.48 us  [the longest x1 2.97 us: local(): far_half = lax.ppermute(half, ('dom', 'edge'), both)]
    unnamed x36 -> x18, local copies, waits for them, and re-layouts: 10.2 us -> 2.48 us
    ppermute x4 -> x2, waiting for transfers between devices: 12.7 us -> 9 us  [the longest x1 6.04 us: local(): far_half = lax.ppermute(half, ('dom', 'edge'), both)]
    all_to_all x1, blocking collectives: 15.6 us -> 17.9 us  [local(): lax.all_to_all(term, 'edge', split_axis=0, concat_axis=0, tiled=True)]
    pallas_call x1, Pallas kernels: 3.13 us -> 4.5 us  [local(): call(edge_kernel, (weight((edges, width), BF16), weight((4, nodes, hid),...]
    pallas_call x1, Pallas kernels: 2.82 us -> 4.1 us  [local(): call(functools.partial(choose_kernel, nodes), weight((4, LANE, groups * L...]
    pallas_call x2 -> x1, Pallas kernels: 3.65 us -> 3.02 us  [local(): call(pick_kernel, (weight((entries, LANE), BF16), weight((packed_rows, hi...]
  transfers between devices with their start and end apart: 9 -> 7, of which waited for: 3 -> 3; matrix products, arithmetic and copies ran while one was open for 1% -> 2% of each run, Pallas kernels for 6% -> 7%
where the time goes in v2:
time: 87.3 us; the launch traced here: 86.8 us
  starting transfers between devices  34.7 us (40%)
  blocking collectives  17.9 us (21%)
  Pallas kernels  14.8 us (17%)
  waiting for transfers between devices  14.5 us (17%)
  local copies, waits for them, and re-layouts  2.52 us (3%)
  other arithmetic  1.5 us (2%)
    all_to_all x1, blocking collectives, local(): lax.all_to_all(term, 'edge', split_axis=0, concat_axis=0, tiled=True)  17.9 us
    all_to_all x1, starting transfers between devices, local(): lax.all_to_all(outgoing.reshape(peers, slots, LANE), 'dom', split_axis=0,...  17.8 us
    ppermute x1, waiting for transfers between devices, local(): far_half = lax.ppermute(half, ('dom', 'edge'), both)  6.04 us
    all_to_all x1, waiting for transfers between devices, local(): lax.all_to_all(chosen, 'edge', split_axis=0, concat_axis=0, tiled=True)  5.5 us
    pallas_call x1, Pallas kernels, local(): call(edge_kernel, (weight((edges, width), BF16), weight((4, nodes, hid),...  4.5 us
    all_to_all x1, starting transfers between devices, local(): lax.all_to_all(chosen, 'edge', split_axis=0, concat_axis=0, tiled=True)  4.14 us
    pallas_call x1, Pallas kernels, local(): call(functools.partial(choose_kernel, nodes), weight((4, LANE, groups * L...  4.1 us
    ppermute x1, starting transfers between devices, local(): near_w = lax.ppermute(own_w, ('dom', 'edge'), both)  3.4 us
  transfers between devices with their start and end apart: 7, of which 3 were waited for; matrix products, arithmetic and copies ran while one was open for 2% of the time, Pallas kernels for 7%

profile of v2, /device:TPU:56, one launch (start us, length us, event | category | flops | bytes accessed | tf_op | source)
XLA Modules:
  0.0 86.8 jit_solution(18302812208810343471)
XLA Ops:
  0.6 3.0 %pick_listed.1 = (bf16[2048,128]{1,0:T(8,128)(2,1)}, bf16[800,512]{1,0:T(8,128)(2,1)S(1)}) custom-call(s32[16,128]{1,0:T(8,128)} %bitcast.18, bf16[256,512]{1,0:T(8,128)(2,1)} %node_ref.3, s32[4,128]{1,0:T(4,128)} %bitcast.12, bf16[128,512]{1,0:T(8,128)(2,1)} %refs_0_.1, bf16[128,512]{1,0:T(8,128)(2,1)} %refs_1_.1, bf16[128,512]{1,0:T(8,128)(2,1)} %refs_2_.1, ...), custom_call_target="tpu_custom_call" | custom-call | flops 335544320 | bytes 786432 | tf_op jit(solution)/shard_map/pick_listed/pallas_call | solution.py:305
  3.7 3.4 %collective-permute-start = (bf16[800,512]{1,0:T(8,128)(2,1)S(1)}, bf16[800,512]{1,0:T(8,128)(2,1)S(1)}, u32[]{:S(2)}, u32[]{:S(2)}) collective-permute-start(bf16[800,512]{1,0:T(8,128)(2,1)S(1)} %get-tuple-element.7.e0.r0.h0.n0), channel_id=1, source_target_pairs={{0,1},{1,2},{2,3},{3,0},{4,7},{5,4},{6,5},{7,6},{8,9},{9,10},{10,1... | collective-permute-start | bytes 2457608 | tf_op jit(solution)/shard_map/send_near/ppermute | solution.py:326
  7.1 17.8 %all-to-all-start = ((bf16[128,16,128]{2,1,0:T(8,128)(2,1)}), bf16[128,16,128]{2,1,0:T(8,128)(2,1)S(1)}, u32[]{:S(2)}, u32[]{:S(2)}) async-start(bf16[128,16,128]{2,1,0:T(8,128)(2,1)} %bitcast.5), calls=%async_computation | async-start | bytes 1048576 | tf_op jit(solution)/shard_map/send_listed/all_to_all | solution.py:328
  24.9 0.0 copy-start.7
  24.9 0.0 collective-permute-done.e1.r1.h1.near_ref.n1
  24.9 3.0 %collective-permute-start.2 = (bf16[400,512]{1,0:T(8,128)(2,1)S(1)}, bf16[400,512]{1,0:T(8,128)(2,1)S(1)}, u32[]{:S(2)}, u32[]{:S(2)}) collective-permute-start(bf16[400,512]{1,0:T(8,128)(2,1)S(1)} %constant_dynamic-slice_fusion), channel_id=1, source_target_pairs={{0,1},{1,2},{2,3},{3,0},{4,7},{5,4},{6,5},{7,6},{8,9},{9,10},{10,1... | collective-permute-start | bytes 1228808 | tf_op jit(solution)/shard_map/send_far/ppermute | solution.py:336
  27.9 2.0 %collective-permute-start.1 = (bf16[800,512]{1,0:T(8,128)(2,1)S(1)}, bf16[800,512]{1,0:T(8,128)(2,1)S(1)}, u32[]{:S(2)}, u32[]{:S(2)}) collective-permute-start(bf16[800,512]{1,0:T(8,128)(2,1)S(1)} %collective-permute-done.e1.r1.h1.near_ref.n1), channel_id=1, source_target_pairs={{0,4},{4,0},{8,12},{12,8},{16,20},{20,16},{24,28},{28,24},{32,36},... | collective-permute-start | bytes 2457608 | tf_op jit(solution)/shard_map/swap_near/ppermute | solution.py:338
  29.9 6.0 %collective-permute-done.2.low_ref.high_ref = bf16[400,512]{1,0:T(8,128)(2,1)S(1)} collective-permute-done((bf16[400,512]{1,0:T(8,128)(2,1)S(1)}, bf16[400,512]{1,0:T(8,128)(2,1)S(1)}, u32[]{:S(2)}, u32[]{:S(2)}) %collective-permute-start.2) | collective-permute-done | bytes 409632 | tf_op jit(solution)/shard_map/send_far/ppermute | solution.py:336
  36.0 0.0 copy-start.4
  36.0 1.9 %collective-permute-start.3 = (bf16[400,512]{1,0:T(8,128)(2,1)S(1)}, bf16[400,512]{1,0:T(8,128)(2,1)}, u32[]{:S(2)}, u32[]{:S(2)}) collective-permute-start(bf16[400,512]{1,0:T(8,128)(2,1)S(1)} %collective-permute-done.2.low_ref.high_ref), channel_id=1, source_target_pairs={{0,4},{4,0},{8,12},{12,8},{16,20},{20,16},{24,28},{28,24},{32,36},... | collective-permute-start | bytes 1228808 | tf_op jit(solution)/shard_map/swap_far/ppermute | solution.py:340
  37.9 0.0 copy-done.7
  37.9 2.5 %collective-permute-start.4 = (s32[4,128]{1,0:T(4,128)S(1)}, s32[4,128]{1,0:T(4,128)S(1)}, u32[]{:S(2)}, u32[]{:S(2)}) collective-permute-start(s32[4,128]{1,0:T(4,128)S(1)} %bitcast.13), channel_id=1, source_target_pairs={{1,0},{2,1},{3,2},{0,3},{7,4},{4,5},{5,6},{6,7},{9,8},{10,9},{11,1... | collective-permute-start | bytes 6152 | tf_op jit(solution)/shard_map/send_slots/ppermute | solution.py:333
  40.4 3.0 %collective-permute-done.4.across_ref = s32[4,128]{1,0:T(4,128)S(1)} collective-permute-done((s32[4,128]{1,0:T(4,128)S(1)}, s32[4,128]{1,0:T(4,128)S(1)}, u32[]{:S(2)}, u32[]{:S(2)}) %collective-permute-start.4) | collective-permute-done | bytes 2080 | tf_op jit(solution)/shard_map/send_slots/ppermute | solution.py:333
  43.4 0.0 all-to-all-done
  43.4 4.1 %choose_senders.1 = bf16[4,128,512]{2,1,0:T(8,128)(2,1)S(1)} custom-call(s32[4,128]{1,0:T(4,128)S(1)} %bitcast.14, s32[4,128]{1,0:T(4,128)S(1)} %collective-permute-done.4.across_ref, bf16[800,512]{1,0:T(8,128)(2,1)S(1)} %collective-permute-done.e1.r1.h1.near_ref.n1, bf16[400,512]{1,0:T(8,128)(2,1)S(1)} %collective-permute-done.2.low_ref.high_ref, ...), custom_call_target="tpu_custom_call" | custom-call | flops 1073741824 | bytes 1048576 | tf_op jit(solution)/shard_map/choose_senders/pallas_call | solution.py:345
  47.5 0.0 copy-done.4
  47.5 0.0 copy-start.5
  47.5 0.8 copy-done.5
  48.3 4.1 %all-to-all-start.1 = ((bf16[4,128,512]{2,1,0:T(8,128)(2,1)}), bf16[4,128,512]{2,1,0:T(8,128)(2,1)}, u32[]{:S(2)}, u32[]{:S(2)}) async-start(bf16[4,128,512]{2,1,0:T(8,128)(2,1)} %copy-done.5), calls=%async_computation.1 | async-start | bytes 1048576 | tf_op jit(solution)/shard_map/send_senders/all_to_all | solution.py:362
  52.5 0.0 copy-start.1
  52.5 0.0 copy-start.3
  52.5 0.0 collective-permute-done.3
  52.5 1.5 %slice_select_fusion = (bf16[384,512]{1,0:T(8,128)(2,1)S(1)}, bf16[384,512]{1,0:T(8,128)(2,1)S(1)}) fusion(bf16[400,512]{1,0:T(8,128)(2,1)} %copy-done.4, bf16[400,512]{1,0:T(8,128)(2,1)} %collective-permute-done.3, pred[]{:T(512)S(6)} %eq.4), kind=kLoop, calls=%fused_computation | loop fusion | flops 393216 | bytes 2359297 | tf_op jit(solution)/shard_map/swap_far/select_n | solution.py:342
  54.0 0.0 collective-permute-done.1.e2.r2.h2.n2
  54.0 0.0 copy-start.6
  54.0 0.0 copy-done.1
  54.0 0.0 copy-done.3
  54.1 0.6 copy-done.6
  54.7 1.8 %edge_pre_local.1.base_hbm = f32[512,512]{1,0:T(8,128)S(1)} custom-call(bf16[512,512]{1,0:T(8,128)(2,1)S(1)} %copy-done.3, bf16[256,512]{1,0:T(8,128)(2,1)S(1)} %copy-done.1, s32[4,128]{1,0:T(4,128)S(1)} %bitcast.15, s32[4,128]{1,0:T(4,128)S(1)} %bitcast.10, bf16[800,512]{1,0:T(8,128)(2,1)S(1)} %get-tuple-element.7.e0.r0.h0.n0, ...), custom_call_target="tpu_custom_call" | custom-call | flops 805306368 | bytes 3145728 | tf_op jit(solution)/shard_map/edge_pre_local/pallas_call | solution.py:371
  56.5 0.0 copy-start
  56.5 1.0 %copy-done = f32[512,512]{1,0:T(8,128)} copy-done((f32[512,512]{1,0:T(8,128)}, f32[512,512]{1,0:T(8,128)S(1)}, u32[]{:S(2)}) %copy-start) | copy-done | bytes 1048600
  57.5 5.5 %all-to-all-done.1.got_ref = bf16[4,128,512]{2,1,0:T(8,128)(2,1)} async-done(((bf16[4,128,512]{2,1,0:T(8,128)(2,1)}), bf16[4,128,512]{2,1,0:T(8,128)(2,1)}, u32[]{:S(2)}, u32[]{:S(2)}) %all-to-all-start.1) | async-done | bytes 524320 | tf_op jit(solution)/shard_map/send_senders/all_to_all | solution.py:362
  63.0 4.5 %edge_update.1 = (bf16[512,512]{1,0:T(8,128)(2,1)}, bf16[4,256,512]{2,1,0:T(8,128)(2,1)S(1)}) custom-call(bf16[512,512]{1,0:T(8,128)(2,1)} %edge_hbm.1, f32[512,512]{1,0:T(8,128)} %copy-done, bf16[256,512]{1,0:T(8,128)(2,1)} %node_ref.3, bf16[128,512]{1,0:T(8,128)(2,1)} %self_hbm.1, f32[1,512]{1,0:T(1,128)} %bitcast.17, ...), custom_call_target="tpu_custom_call" | custom-call | flops 805306368 | bytes 4194304 | tf_op jit(solution)/shard_map/edge_update/pallas_call | solution.py:384
  67.5 0.0 copy-start.2
  67.5 0.0 copy-start.8
  67.5 17.9 %all_to_all.15.terms_ref = bf16[4,256,512]{2,1,0:T(8,128)(2,1)S(1)} all-to-all(bf16[4,256,512]{2,1,0:T(8,128)(2,1)S(1)} %get-tuple-element.10), channel_id=1, replica_groups=mesh['dom'=128,'edge'=4] {'edge'}, dimensions={0} | all-to-all | bytes 2097152 | tf_op jit(solution)/shard_map/send_terms/all_to_all | solution.py:408
  85.4 0.0 copy-done.2
  85.4 0.0 copy-done.8
  85.4 1.4 %node_update.1 = bf16[256,512]{1,0:T(8,128)(2,1)} custom-call(bf16[4,256,512]{2,1,0:T(8,128)(2,1)S(1)} %all_to_all.15.terms_ref, bf16[256,512]{1,0:T(8,128)(2,1)S(1)} %copy-done.2, f32[1,512]{1,0:T(1,128)S(1)} %bitcast.16, bf16[800,512]{1,0:T(8,128)(2,1)S(1)} %get-tuple-element.7.e0.r0.h0.n0, bf16[800,512]{1,0:T(8,128)(2,1)S(1)} %collective-permute-done.e1.r1.h1.near_ref.n1, ...), custom_call_target="tpu_custom_call" | custom-call | flops 134217728 | bytes 2097152 | tf_op jit(solution)/shard_map/node_update/pallas_call | solution.py:411
  (1 shorter events, 0.0 us)
Async XLA Ops:
  3.7 21.2 %collective-permute-start = (bf16[800,512]{1,0:T(8,128)(2,1)S(1)}, bf16[800,512]{1,0:T(8,128)(2,1)S(1)}, u32[]{:S(2)}, u32[]{:S(2)}) collective-permute-start(bf16[800,512]{1,0:T(8,128)(2,1)S(1)} %get-tuple-element.7.e0.r0.h0.n0), channel_id=1, source_target_pairs={{0,1},{1,2},{2,3},{3,0},{4,7},{5,4},{6,5},{7,6},{8,9},{9,10},{10,1... | collective-permute-start | bytes 2457608 | tf_op jit(solution)/shard_map/send_near/ppermute | solution.py:326
  7.1 36.3 %all-to-all-start = ((bf16[128,16,128]{2,1,0:T(8,128)(2,1)}), bf16[128,16,128]{2,1,0:T(8,128)(2,1)S(1)}, u32[]{:S(2)}, u32[]{:S(2)}) async-start(bf16[128,16,128]{2,1,0:T(8,128)(2,1)} %bitcast.5), calls=%async_computation | async-start | bytes 1048576 | tf_op jit(solution)/shard_map/send_listed/all_to_all | solution.py:328
  24.9 13.0 %copy-start.7 = (s32[512]{0:T(512)S(1)}, s32[512]{0:T(512)}, u32[]{:S(2)}) copy-start(s32[512]{0:T(512)} %param.16) | copy-start | bytes 6148
  24.9 11.1 %collective-permute-start.2 = (bf16[400,512]{1,0:T(8,128)(2,1)S(1)}, bf16[400,512]{1,0:T(8,128)(2,1)S(1)}, u32[]{:S(2)}, u32[]{:S(2)}) collective-permute-start(bf16[400,512]{1,0:T(8,128)(2,1)S(1)} %constant_dynamic-slice_fusion), channel_id=1, source_target_pairs={{0,1},{1,2},{2,3},{3,0},{4,7},{5,4},{6,5},{7,6},{8,9},{9,10},{10,1... | collective-permute-start | bytes 1228808 | tf_op jit(solution)/shard_map/send_far/ppermute | solution.py:336
  27.9 26.1 %collective-permute-start.1 = (bf16[800,512]{1,0:T(8,128)(2,1)S(1)}, bf16[800,512]{1,0:T(8,128)(2,1)S(1)}, u32[]{:S(2)}, u32[]{:S(2)}) collective-permute-start(bf16[800,512]{1,0:T(8,128)(2,1)S(1)} %collective-permute-done.e1.r1.h1.near_ref.n1), channel_id=1, source_target_pairs={{0,4},{4,0},{8,12},{12,8},{16,20},{20,16},{24,28},{28,24},{32,36},... | collective-permute-start | bytes 2457608 | tf_op jit(solution)/shard_map/swap_near/ppermute | solution.py:338
  36.0 11.5 %copy-start.4 = (bf16[400,512]{1,0:T(8,128)(2,1)}, bf16[400,512]{1,0:T(8,128)(2,1)S(1)}, u32[]{:S(2)}) copy-start(bf16[400,512]{1,0:T(8,128)(2,1)S(1)} %collective-permute-done.2.low_ref.high_ref) | copy-start | bytes 1228804
  36.0 16.5 %collective-permute-start.3 = (bf16[400,512]{1,0:T(8,128)(2,1)S(1)}, bf16[400,512]{1,0:T(8,128)(2,1)}, u32[]{:S(2)}, u32[]{:S(2)}) collective-permute-start(bf16[400,512]{1,0:T(8,128)(2,1)S(1)} %collective-permute-done.2.low_ref.high_ref), channel_id=1, source_target_pairs={{0,4},{4,0},{8,12},{12,8},{16,20},{20,16},{24,28},{28,24},{32,36},... | collective-permute-start | bytes 1228808 | tf_op jit(solution)/shard_map/swap_far/ppermute | solution.py:340
  37.9 5.5 %collective-permute-start.4 = (s32[4,128]{1,0:T(4,128)S(1)}, s32[4,128]{1,0:T(4,128)S(1)}, u32[]{:S(2)}, u32[]{:S(2)}) collective-permute-start(s32[4,128]{1,0:T(4,128)S(1)} %bitcast.13), channel_id=1, source_target_pairs={{1,0},{2,1},{3,2},{0,3},{7,4},{4,5},{5,6},{6,7},{9,8},{10,9},{11,1... | collective-permute-start | bytes 6152 | tf_op jit(solution)/shard_map/send_slots/ppermute | solution.py:333
  47.5 0.8 copy-start.5
  48.3 14.7 %all-to-all-start.1 = ((bf16[4,128,512]{2,1,0:T(8,128)(2,1)}), bf16[4,128,512]{2,1,0:T(8,128)(2,1)}, u32[]{:S(2)}, u32[]{:S(2)}) async-start(bf16[4,128,512]{2,1,0:T(8,128)(2,1)} %copy-done.5), calls=%async_computation.1 | async-start | bytes 1048576 | tf_op jit(solution)/shard_map/send_senders/all_to_all | solution.py:362
  52.5 1.6 %copy-start.1 = (bf16[256,512]{1,0:T(8,128)(2,1)S(1)}, bf16[256,512]{1,0:T(8,128)(2,1)}, u32[]{:S(2)}) copy-start(bf16[256,512]{1,0:T(8,128)(2,1)} %node_ref.3) | copy-start | bytes 786436
  52.5 1.6 %copy-start.3 = (bf16[512,512]{1,0:T(8,128)(2,1)S(1)}, bf16[512,512]{1,0:T(8,128)(2,1)}, u32[]{:S(2)}) copy-start(bf16[512,512]{1,0:T(8,128)(2,1)} %edge_hbm.1) | copy-start | bytes 1572868
  54.0 0.7 copy-start.6
  56.5 1.0 %copy-start = (f32[512,512]{1,0:T(8,128)}, f32[512,512]{1,0:T(8,128)S(1)}, u32[]{:S(2)}) copy-start(f32[512,512]{1,0:T(8,128)S(1)} %edge_pre_local.1.base_hbm) | copy-start | bytes 3145732
  67.5 17.9 %copy-start.2 = (bf16[256,512]{1,0:T(8,128)(2,1)S(1)}, bf16[256,512]{1,0:T(8,128)(2,1)}, u32[]{:S(2)}) copy-start(bf16[256,512]{1,0:T(8,128)(2,1)} %node_ref.3) | copy-start | bytes 786436
  67.5 17.9 %copy-start.8 = (f32[512]{0:T(512)S(1)}, f32[512]{0:T(512)}, u32[]{:S(2)}) copy-start(f32[512]{0:T(512)} %param.27) | copy-start | bytes 6148

commit v3 on v2

v3 whole, which is shorter than its diff:
```python
import jax
import jax.numpy as jnp
from jax import lax
from jax.experimental import pallas as pl
from jax.experimental.pallas import tpu as pltpu
from jax.sharding import PartitionSpec as P

F32 = jnp.float32
BF16 = jnp.bfloat16
LANE = 128
VMEM_BYTES = 24 * 1024 * 1024

W_NODE, W_EDGE, W_RECV, W_SEND, W_OUT, W_AGG = range(6)
HALF = 3
NOTE = 16


def whole():
    return pl.BlockSpec(memory_space=pltpu.VMEM)


def in_hbm(*arrays):
    return [pltpu.with_memory_space_constraint(a, pltpu.HBM) for a in arrays]


def in_vmem(*arrays):
    return [pltpu.with_memory_space_constraint(a, pltpu.VMEM) for a in arrays]


def call(body, outs, in_specs, flops, nbytes, scratch=(), out_specs=None):
    return pl.pallas_call(
        body,
        out_shape=outs,
        in_specs=in_specs,
        out_specs=out_specs
        if out_specs is not None
        else jax.tree.map(lambda o: whole(), outs),
        scratch_shapes=scratch,
        compiler_params=pltpu.CompilerParams(vmem_limit_bytes=VMEM_BYTES),
        cost_estimate=pl.CostEstimate(flops=flops, bytes_accessed=nbytes, transcendentals=0),
    )


def silu(v):
    return 0.5 * v * (1.0 + jnp.tanh(0.5 * v))


def normalize(v):
    center = v - jnp.mean(v, axis=-1, keepdims=True)
    spread = jnp.mean(center * center, axis=-1, keepdims=True)
    return center * lax.rsqrt(spread + 1e-05)


def dot(a, b):
    return jnp.dot(a, b, preferred_element_type=F32)


def shard_order():
    x = lax.axis_index("edge")
    core = lax.rem(lax.axis_index("dom"), 2)
    step = jnp.where(core == 0, 3, 1)
    return (x, lax.rem(x + step, 4), lax.rem(x + 4 - step, 4), lax.rem(x + 2, 4))


def columns(j):
    return pl.ds(pl.multiple_of(j * LANE, LANE), LANE)


def by_shard(ref, rows, order):
    return jnp.concatenate([ref[rows, columns(j)] for j in order], axis=1)


def stacked(place, own_ref, near_ref, across_ref, far_ref, far_across_ref):
    at = place * LANE + (NOTE if place >= HALF else 0)
    parts = [r[at : at + LANE, :] for r in (own_ref, near_ref, across_ref)]
    high = place >= HALF
    at = (place % HALF) * LANE + (NOTE if high else 0)
    here = lax.rem(lax.axis_index("dom"), 2) == (1 if high else 0)
    rows = slice(at, at + LANE)
    parts.append(jnp.where(here, far_ref[rows, :], far_across_ref[rows, :]))
    return jnp.concatenate(parts, axis=0)


def column_of(row_block):
    return jnp.transpose(row_block.astype(F32))


def pick_kernel(listed_hbm, node_hbm, slot_hbm, *refs):
    shards = refs[:6]
    out_hbm, packed, listed_ref, node_ref, slot_ref, stage_ref, out_ref, sem = refs[6:]
    part, hid = shards[0].shape
    mine = columns(lax.axis_index("edge"))
    first = [
        pltpu.make_async_copy(listed_hbm, listed_ref, sem.at[0]),
        pltpu.make_async_copy(node_hbm.at[:, mine], node_ref, sem.at[1]),
        pltpu.make_async_copy(slot_hbm, slot_ref, sem.at[2]),
    ]
    copies = []
    for k, shard in enumerate(shards):
        at = k * part + (NOTE if k >= HALF else 0)
        copies.append(pltpu.make_async_copy(shard, packed.at[at : at + part, :], sem.at[3 + k]))
    for c in first + copies:
        c.start()
    slots, peers = listed_ref.shape
    nodes = node_ref.shape[0]
    node = lax.broadcasted_iota(jnp.int32, (1, nodes), 1).astype(F32)
    first[0].wait()
    listed = column_of(listed_ref[...])
    first[1].wait()
    chunk = min(32, peers)
    rows = chunk * slots
    for k, peer in enumerate(range(0, peers, chunk)):
        at = peer * slots
        onehot = jnp.concatenate(
            [
                jnp.where(
                    jnp.broadcast_to(listed[peer : peer + chunk, s : s + 1], (chunk, nodes)) == node,
                    1.0,
                    0.0,
                ).astype(BF16)
                for s in range(slots)
            ],
            axis=0,
        )
        found = dot(onehot, node_ref[...])
        for s in range(slots):
            stage_ref[pl.ds(at + s, chunk, stride=slots), :] = found[s * chunk : (s + 1) * chunk, :]
        out_ref[at : at + rows, :] = stage_ref[at : at + rows, :].astype(BF16)
        copies.append(
            pltpu.make_async_copy(
                out_ref.at[at : at + rows, :], out_hbm.at[at : at + rows, :], sem.at[9 + k]
            )
        )
        copies[-1].start()
    first[2].wait()
    groups = slot_ref.shape[0]
    high = lax.shift_right_logical(slot_ref[...], 4)
    low = jnp.bitwise_and(slot_ref[...], 15)
    note = jnp.concatenate(
        [v.astype(F32) for v in (high, low)] + [jnp.zeros((groups, hid - 2 * LANE), F32)], axis=1
    )
    note = jnp.concatenate([note, jnp.zeros((NOTE - groups, hid), F32)], axis=0).astype(BF16)
    for at in (HALF * part, 2 * HALF * part + NOTE):
        packed[at : at + NOTE, :] = note
    for c in copies:
        c.wait()


def noted(block, groups):
    v = block[:, 0 : 2 * LANE].astype(F32)
    return (v[:groups, :LANE] * 16.0 + v[:groups, LANE:]).astype(jnp.int32)


def choose_kernel(
    own_ref, across_ref, near_ref, far_ref, node_ref, table_hbm, out_ref, table_ref, sem
):
    nodes = node_ref.shape[0]
    half = (nodes + table_hbm.shape[0]) // 2
    split = max(half - nodes, 0)
    skip = nodes + split - half
    parts = [(table_hbm.at[split:, :], table_ref.at[skip:, LANE:])]
    if split:
        parts.append((table_hbm.at[:split, :], table_ref.at[nodes:, :LANE]))
    copies = [pltpu.make_async_copy(a, b, sem.at[k]) for k, (a, b) in enumerate(parts)]
    for c in copies:
        c.start()
    mine = node_ref[:, columns(lax.axis_index("edge"))]
    table_ref[: min(nodes, half), :LANE] = mine[: min(nodes, half), :]
    if skip:
        table_ref[:skip, LANE:] = mine[half:, :]
    order = shard_order()
    groups = own_ref.shape[0]
    core = lax.rem(lax.axis_index("dom"), 2)
    middle = slice(HALF * LANE, HALF * LANE + NOTE)
    far = jnp.where(core == 0, far_ref[middle, :].astype(F32), far_ref[0:NOTE, :].astype(F32))
    slots = jnp.concatenate(
        [own_ref[...], noted(near_ref[middle, :], groups), across_ref[...], noted(far, groups)],
        axis=0,
    )
    wanted = column_of(slots)
    second = wanted >= float(half)
    wanted = jnp.where(second, wanted - float(half), wanted)
    second = jnp.where(second, 1.0, 0.0)
    step = LANE if half % LANE == 0 else half
    for c in copies:
        c.wait()
    lane = lax.broadcasted_iota(jnp.int32, (1, step), 1).astype(F32)
    for k in range(4):
        for g in range(groups):
            at = k * groups + g
            place = jnp.broadcast_to(wanted[:, at : at + 1], (LANE, step))
            onehot = jnp.concatenate(
                [
                    jnp.where(place == lane + float(base), 1.0, 0.0).astype(BF16)
                    for base in range(0, half, step)
                ],
                axis=1,
            )
            found = dot(onehot, table_ref[...])
            later = jnp.broadcast_to(second[:, at : at + 1], (LANE, LANE)) > 0.5
            found = jnp.where(later, found[:, LANE:], found[:, :LANE])
            out_ref[order[k], :, g * LANE : (g + 1) * LANE] = found.astype(BF16)


def edge_kernel(
    edge_ref, node_ref, self_ref, gain_hbm, got_ref, recv_ref,
    own_w, near_w, across_w, far_w, far_across_w,
    out_ref, term_ref, hidden_ref, message_ref, total_ref, gain_ref, sem,
):
    gain_in = pltpu.make_async_copy(gain_hbm, gain_ref, sem)
    gain_in.start()
    order = shard_order()
    edges = edge_ref.shape[0]
    nodes = node_ref.shape[0]
    blocks = [slice(g * LANE, (g + 1) * LANE) for g in range(edges // LANE)]
    shards = (own_w, near_w, across_w, far_w, far_across_w)
    at_node = dot(by_shard(node_ref, slice(None), order), stacked(W_RECV, *shards)).astype(BF16)
    w_edge = stacked(W_EDGE, *shards)
    w_send = stacked(W_SEND, *shards)
    recv = column_of(recv_ref[...])
    lane = lax.broadcasted_iota(jnp.int32, (1, nodes), 1).astype(F32)
    for g, rows in enumerate(blocks):
        sender = jnp.concatenate([got_ref[j, :, rows] for j in order], axis=1)
        place = jnp.broadcast_to(recv[:, g : g + 1], (LANE, nodes))
        onehot = jnp.where(place == lane, 1.0, 0.0).astype(BF16)
        before = dot(by_shard(edge_ref, rows, order), w_edge) + dot(sender, w_send)
        hidden_ref[rows, :] = silu(before + dot(onehot, at_node)).astype(BF16)
    w_out = stacked(W_OUT, *shards)
    gain_in.wait()
    for rows in blocks:
        message = normalize(dot(by_shard(hidden_ref, rows, order), w_out)) * gain_ref[...]
        out_ref[rows, :] = (edge_ref[rows, :].astype(F32) + message).astype(BF16)
        message_ref[rows, :] = message.astype(BF16)
    node = lax.broadcasted_iota(jnp.int32, (nodes, LANE), 0)
    onehot = jnp.concatenate(
        [
            jnp.where(recv_ref[g : g + 1, :] == node, 1.0, 0.0).astype(BF16)
            for g in range(len(blocks))
        ],
        axis=1,
    )
    total_ref[...] = dot(onehot, message_ref[...]).astype(BF16)
    term = dot(by_shard(total_ref, slice(None), order), stacked(W_AGG, *shards))
    own = node_ref[:, columns(lax.axis_index("edge"))]
    term = (term + dot(own, self_ref[...])).astype(BF16)
    for j in range(term_ref.shape[0]):
        term_ref[j] = term


def node_kernel(
    terms_ref, node_ref, gain_ref, own_w, near_w, across_w, far_w, far_across_w,
    out_ref, hidden_ref,
):
    order = shard_order()
    terms = [terms_ref[j].astype(F32) for j in range(terms_ref.shape[0])]
    hidden_ref[...] = silu((terms[0] + terms[1]) + (terms[2] + terms[3])).astype(BF16)
    update = normalize(
        dot(
            by_shard(hidden_ref, slice(None), order),
            stacked(W_NODE, own_w, near_w, across_w, far_w, far_across_w),
        )
    )
    out_ref[...] = (node_ref[...].astype(F32) + update * gain_ref[...]).astype(BF16)


def local(
    node_feat, edge_feat, edge_slot, edge_recv, send_list, edge_w_edge, edge_w_send, edge_w_recv,
    edge_w_out, edge_gain, node_w_self, node_w_agg, node_w_out, node_gain,
):
    peers = lax.axis_size("dom")
    core = lax.rem(lax.axis_index("dom"), 2)
    nodes, width = node_feat.shape
    edges = edge_feat.shape[0]
    part, hid = edge_w_edge.shape
    slots = send_list.shape[2]
    entries = peers * slots
    groups = edges // LANE
    weight = jax.ShapeDtypeStruct

    both = [
        (d * 4 + i, d * 4 + (i + (1 if d % 2 == 0 else 3)) % 4)
        for d in range(peers)
        for i in range(4)
    ]
    back = [(i, j) for j, i in both]
    swap = [(d, d ^ 1) for d in range(peers)]

    anywhere = pl.BlockSpec(memory_space=pltpu.HBM)
    dma = pltpu.SemaphoreType.DMA
    own_slot = edge_slot.reshape(groups, LANE)
    recv = edge_recv.reshape(groups, LANE)
    packed_rows = 2 * (HALF * part + NOTE)
    half_rows = HALF * part + NOTE

    with jax.named_scope("pick_listed"):
        outgoing, own_w = call(
            pick_kernel,
            (pltpu.HBM((entries, LANE), BF16), weight((packed_rows, hid), BF16)),
            [anywhere] * 9,
            2 * entries * 640 * LANE,
            entries * 256 + nodes * width * 2,
            scratch=[
                pltpu.VMEM((slots, peers), jnp.int32),
                pltpu.VMEM((nodes, LANE), BF16),
                pltpu.VMEM((groups, LANE), jnp.int32),
                pltpu.VMEM((entries, LANE), F32),
                pltpu.VMEM((entries, LANE), BF16),
                dma((9 + max(1, peers // 32),)),
            ],
            out_specs=(anywhere, whole()),
        )(
            *in_hbm(
                send_list[0].T, node_feat, own_slot,
                node_w_out, edge_w_edge, edge_w_recv, edge_w_send, edge_w_out, node_w_agg,
            )
        )
    with jax.named_scope("send_near"):
        near_w = lax.ppermute(own_w, ("dom", "edge"), both)
    with jax.named_scope("send_listed"):
        arrived = lax.all_to_all(
            outgoing.reshape(peers, slots, LANE), "dom", split_axis=0, concat_axis=0, tiled=True
        )
    with jax.named_scope("send_slots"):
        half = lax.dynamic_slice_in_dim(near_w, HALF * part * core, half_rows, 0)
        half, back_slot = lax.optimization_barrier((half, own_slot))
        across_slot = lax.ppermute(back_slot, ("dom", "edge"), back)
    with jax.named_scope("send_far"):
        far_half = lax.ppermute(half, ("dom", "edge"), both)
    with jax.named_scope("swap_near"):
        near_again, across_slot = lax.optimization_barrier((near_w, across_slot))
        across_w = lax.ppermute(near_again, "dom", swap)
    with jax.named_scope("swap_far"):
        across_half = lax.ppermute(far_half, "dom", swap)
    shards = (own_w, near_w, across_w, far_half, across_half)

    with jax.named_scope("choose_senders"):
        chosen = call(
            choose_kernel,
            weight((4, LANE, groups * LANE), BF16),
            [whole()] * 5 + [anywhere],
            2 * 2 * edges * entries * LANE,
            entries * LANE * 2 + 4 * edges * LANE * 2,
            scratch=[pltpu.VMEM(((nodes + entries) // 2, 2 * LANE), BF16), dma((2,))],
        )(own_slot, across_slot, near_w, far_half, node_feat, arrived.reshape(entries, LANE))
    with jax.named_scope("send_senders"):
        got = lax.all_to_all(chosen, "edge", split_axis=0, concat_axis=0, tiled=True)
    with jax.named_scope("edge_update"):
        edge_out, term = call(
            edge_kernel,
            (weight((edges, width), BF16), weight((4, nodes, hid), BF16)),
            [whole()] * 3 + [anywhere] + [whole()] * 7,
            2 * (2 * edges + 2 * nodes) * width * hid,
            edges * width * 10 + 3 * width * hid * 2,
            scratch=[
                pltpu.VMEM((edges, hid), BF16),
                pltpu.VMEM((edges, width), BF16),
                pltpu.VMEM((nodes, width), BF16),
                pltpu.VMEM((1, width), F32),
                dma(()),
            ],
        )(
            *in_vmem(edge_feat, node_feat, node_w_self), *in_hbm(edge_gain.reshape(1, width)),
            got, *in_vmem(recv), *shards,
        )
    with jax.named_scope("send_terms"):
        terms = lax.all_to_all(term, "edge", split_axis=0, concat_axis=0, tiled=True)
    with jax.named_scope("node_update"):
        node_out = call(
            node_kernel,
            weight((nodes, width), BF16),
            [whole()] * 8,
            2 * nodes * width * hid,
            nodes * width * 12 + width * hid * 2,
            scratch=[pltpu.VMEM((nodes, hid), BF16)],
        )(terms, node_feat, node_gain.reshape(1, width), *shards)
    return (node_out, edge_out)


def solution(mesh):
    in_specs = (
        P("dom", None),
        P(("dom", "edge"), None),
        P(("dom", "edge")),
        P(("dom", "edge")),
        P("dom", None, None),
        P("edge", None),
        P("edge", None),
        P("edge", None),
        P("edge", None),
        P(),
        P("edge", None),
        P("edge", None),
        P("edge", None),
        P(),
    )
    out_specs = (P("dom", None), P(("dom", "edge"), None))
    return jax.shard_map(local, mesh=mesh, in_specs=in_specs, out_specs=out_specs, check_vma=False)
```

time: 87.3 us -> 82.1 us (0.940)
  blocking collectives: 17.9 us -> 31.3 us
  waiting for transfers between devices: 14.5 us -> 5.94 us
  Pallas kernels: 14.8 us -> 9.63 us
  local copies, waits for them, and re-layouts: 2.52 us -> 0.72 us
  other arithmetic: 1.5 us -> 0 us
  starting transfers between devices: 34.7 us -> 33.2 us
    all_to_all x0 -> x1, blocking collectives: none -> 13.9 us  [local(): lax.all_to_all(chosen, 'edge', split_axis=0, concat_axis=0, tiled=True)]
    ppermute x1, waiting for transfers between devices: 6.04 us -> 0.04 us  [local(): far_half = lax.ppermute(half, ('dom', 'edge'), both)]
    all_to_all x1 -> x0, waiting for transfers between devices: 5.5 us -> none  [local(): lax.all_to_all(chosen, 'edge', split_axis=0, concat_axis=0, tiled=True)]
    all_to_all x1, waiting for transfers between devices: 0.01 us -> 4.43 us  [local(): lax.all_to_all(outgoing.reshape(peers, slots, LANE), 'dom', split_axis=0,...]
    all_to_all x1 -> x0, starting transfers between devices: 4.14 us -> none  [local(): lax.all_to_all(chosen, 'edge', split_axis=0, concat_axis=0, tiled=True)]
    pallas_call x4 -> x3, Pallas kernels: 10.3 us -> 6.33 us  [the longest x1 2.64 us: local(): call(choose_kernel, weight((4, LANE, groups * LANE), BF16), [whole()] * 5...]
    unnamed x18 -> x12, local copies, waits for them, and re-layouts: 2.48 us -> 0.68 us
    ppermute x1, starting transfers between devices: 2.51 us -> 4.08 us  [local(): across_slot = lax.ppermute(back_slot, ('dom', 'edge'), back)]
  transfers between devices with their start and end apart: 7 -> 6, of which waited for: 3 -> 2; matrix products, arithmetic and copies ran while one was open for 2% -> 0% of each run, Pallas kernels for 7% -> 3%
where the time goes in v3:
time: 82.1 us; the launch traced here: 81.6 us
  starting transfers between devices  33.2 us (40%)
  blocking collectives  31.3 us (38%)
  Pallas kernels  9.63 us (12%)
  waiting for transfers between devices  5.94 us (7%)
    all_to_all x1, starting transfers between devices, local(): lax.all_to_all(outgoing.reshape(peers, slots, LANE), 'dom', split_axis=0,...  18.2 us
    all_to_all x1, blocking collectives, local(): lax.all_to_all(term, 'edge', split_axis=0, concat_axis=0, tiled=True)  17.4 us
    all_to_all x1, blocking collectives, local(): lax.all_to_all(chosen, 'edge', split_axis=0, concat_axis=0, tiled=True)  13.9 us
    all_to_all x1, waiting for transfers between devices, local(): lax.all_to_all(outgoing.reshape(peers, slots, LANE), 'dom', split_axis=0,...  4.43 us
    ppermute x1, starting transfers between devices, local(): across_slot = lax.ppermute(back_slot, ('dom', 'edge'), back)  4.08 us
    ppermute x1, starting transfers between devices, local(): near_w = lax.ppermute(own_w, ('dom', 'edge'), both)  3.4 us
    pallas_call x1, Pallas kernels, local(): call(edge_kernel, (weight((edges, width), BF16), weight((4, nodes, hid),...  3.3 us
    ppermute x1, starting transfers between devices, local(): far_half = lax.ppermute(half, ('dom', 'edge'), both)  3.1 us
  transfers between devices with their start and end apart: 6, of which 2 were waited for; matrix products, arithmetic and copies ran while one was open for 0% of the time, Pallas kernels for 3%

profile of v3, /device:TPU:56, one launch (start us, length us, event | category | flops | bytes accessed | tf_op | source)
XLA Modules:
  0.0 81.6 jit_solution(9775225678954369705)
XLA Ops:
  0.6 2.3 %pick_listed.1 = (bf16[2048,128]{1,0:T(8,128)(2,1)}, bf16[800,512]{1,0:T(8,128)(2,1)S(1)}) custom-call(s32[16,128]{1,0:T(8,128)} %bitcast.16, bf16[256,512]{1,0:T(8,128)(2,1)} %node_ref.5, s32[4,128]{1,0:T(4,128)} %bitcast.9, bf16[128,512]{1,0:T(8,128)(2,1)} %refs_0_.1, bf16[128,512]{1,0:T(8,128)(2,1)} %refs_1_.1, bf16[128,512]{1,0:T(8,128)(2,1)} %refs_2_.1, ...), custom_call_target="tpu_custom_call" | custom-call | flops 335544320 | bytes 786432 | tf_op jit(solution)/shard_map/pick_listed/pallas_call | solution.py:296
  3.0 3.4 %collective-permute-start = (bf16[800,512]{1,0:T(8,128)(2,1)S(1)}, bf16[800,512]{1,0:T(8,128)(2,1)S(1)}, u32[]{:S(2)}, u32[]{:S(2)}) collective-permute-start(bf16[800,512]{1,0:T(8,128)(2,1)S(1)} %get-tuple-element.10.own_w), channel_id=1, source_target_pairs={{0,1},{1,2},{2,3},{3,0},{4,7},{5,4},{6,5},{7,6},{8,9},{9,10},{10,1... | collective-permute-start | bytes 2457608 | tf_op jit(solution)/shard_map/send_near/ppermute | solution.py:318
  6.4 18.2 %all-to-all-start = ((bf16[128,16,128]{2,1,0:T(8,128)(2,1)}), bf16[128,16,128]{2,1,0:T(8,128)(2,1)}, u32[]{:S(2)}, u32[]{:S(2)}) async-start(bf16[128,16,128]{2,1,0:T(8,128)(2,1)} %bitcast.14), calls=%async_computation | async-start | bytes 1048576 | tf_op jit(solution)/shard_map/send_listed/all_to_all | solution.py:320
  24.6 0.0 copy-start.3
  24.6 0.0 copy-start
  24.6 0.0 collective-permute-done.near_ref.near_w
  24.7 3.1 %collective-permute-start.2 = (bf16[400,512]{1,0:T(8,128)(2,1)S(1)}, bf16[400,512]{1,0:T(8,128)(2,1)S(1)}, u32[]{:S(2)}, u32[]{:S(2)}) collective-permute-start(bf16[400,512]{1,0:T(8,128)(2,1)S(1)} %constant_dynamic-slice_fusion), channel_id=1, source_target_pairs={{0,1},{1,2},{2,3},{3,0},{4,7},{5,4},{6,5},{7,6},{8,9},{9,10},{10,1... | collective-permute-start | bytes 1228808 | tf_op jit(solution)/shard_map/send_far/ppermute | solution.py:328
  27.8 0.0 copy-done.3
  27.8 4.1 %collective-permute-start.1 = (s32[4,128]{1,0:T(4,128)S(1)}, s32[4,128]{1,0:T(4,128)S(1)}, u32[]{:S(2)}, u32[]{:S(2)}) collective-permute-start(s32[4,128]{1,0:T(4,128)S(1)} %bitcast.10), channel_id=1, source_target_pairs={{1,0},{2,1},{3,2},{0,3},{7,4},{4,5},{5,6},{6,7},{9,8},{10,9},{11,1... | collective-permute-start | bytes 6152 | tf_op jit(solution)/shard_map/send_slots/ppermute | solution.py:326
  31.9 1.5 %collective-permute-done.1.across_ref = s32[4,128]{1,0:T(4,128)S(1)} collective-permute-done((s32[4,128]{1,0:T(4,128)S(1)}, s32[4,128]{1,0:T(4,128)S(1)}, u32[]{:S(2)}, u32[]{:S(2)}) %collective-permute-start.1) | collective-permute-done | bytes 2080 | tf_op jit(solution)/shard_map/send_slots/ppermute | solution.py:326
  33.4 2.5 %collective-permute-start.3 = (bf16[800,512]{1,0:T(8,128)(2,1)S(1)}, bf16[800,512]{1,0:T(8,128)(2,1)S(1)}, u32[]{:S(2)}, u32[]{:S(2)}) collective-permute-start(bf16[800,512]{1,0:T(8,128)(2,1)S(1)} %collective-permute-done.near_ref.near_w), channel_id=1, source_target_pairs={{0,4},{4,0},{8,12},{12,8},{16,20},{20,16},{24,28},{28,24},{32,36},... | collective-permute-start | bytes 2457608 | tf_op jit(solution)/shard_map/swap_near/ppermute | solution.py:331
  35.9 0.0 collective-permute-done.2.far_ref.far_w
  35.9 1.9 %collective-permute-start.4 = (bf16[400,512]{1,0:T(8,128)(2,1)S(1)}, bf16[400,512]{1,0:T(8,128)(2,1)S(1)}, u32[]{:S(2)}, u32[]{:S(2)}) collective-permute-start(bf16[400,512]{1,0:T(8,128)(2,1)S(1)} %collective-permute-done.2.far_ref.far_w), channel_id=1, source_target_pairs={{0,4},{4,0},{8,12},{12,8},{16,20},{20,16},{24,28},{28,24},{32,36},... | collective-permute-start | bytes 1228808 | tf_op jit(solution)/shard_map/swap_far/ppermute | solution.py:333
  37.8 4.4 %all-to-all-done = bf16[128,16,128]{2,1,0:T(8,128)(2,1)} async-done(((bf16[128,16,128]{2,1,0:T(8,128)(2,1)}), bf16[128,16,128]{2,1,0:T(8,128)(2,1)}, u32[]{:S(2)}, u32[]{:S(2)}) %all-to-all-start) | async-done | bytes 524320 | tf_op jit(solution)/shard_map/send_listed/all_to_all | solution.py:320
  42.3 0.0 copy-done
  42.3 2.6 %choose_senders.1 = bf16[4,128,512]{2,1,0:T(8,128)(2,1)S(1)} custom-call(s32[4,128]{1,0:T(4,128)S(1)} %bitcast.11, s32[4,128]{1,0:T(4,128)S(1)} %collective-permute-done.1.across_ref, bf16[800,512]{1,0:T(8,128)(2,1)S(1)} %collective-permute-done.near_ref.near_w, bf16[400,512]{1,0:T(8,128)(2,1)S(1)} %collective-permute-done.2.far_ref.far_w, ...), custom_call_target="tpu_custom_call" | custom-call | flops 536870912 | bytes 1048576 | tf_op jit(solution)/shard_map/choose_senders/pallas_call | solution.py:337
  44.9 0.0 copy-start.1
  44.9 0.0 copy-start.2
  44.9 13.9 %all_to_all.15.got_ref = bf16[4,128,512]{2,1,0:T(8,128)(2,1)S(1)} all-to-all(bf16[4,128,512]{2,1,0:T(8,128)(2,1)S(1)} %choose_senders.1), channel_id=1, replica_groups=mesh['dom'=128,'edge'=4] {'edge'}, dimensions={0} | all-to-all | bytes 1048576 | tf_op jit(solution)/shard_map/send_senders/all_to_all | solution.py:346
  58.9 0.0 copy-start.4
  58.9 0.0 collective-permute-done.4.far_across_w
  58.9 0.0 collective-permute-done.3.across_w
  58.9 0.0 copy-done.1
  58.9 0.0 copy-done.2
  58.9 0.7 copy-done.4
  59.6 3.3 %edge_update.1 = (bf16[512,512]{1,0:T(8,128)(2,1)}, bf16[4,256,512]{2,1,0:T(8,128)(2,1)S(1)}) custom-call(bf16[512,512]{1,0:T(8,128)(2,1)S(1)} %copy-done.1, bf16[256,512]{1,0:T(8,128)(2,1)S(1)} %copy-done, bf16[128,512]{1,0:T(8,128)(2,1)S(1)} %copy-done.2, f32[1,512]{1,0:T(1,128)} %bitcast.15, bf16[4,128,512]{2,1,0:T(8,128)(2,1)S(1)} %all_to_all.15.got_ref, ...), custom_call_target="tpu_custom_call" | custom-call | flops 805306368 | bytes 4194304 | tf_op jit(solution)/shard_map/edge_update/pallas_call | solution.py:348
  62.9 0.0 copy-start.5
  62.9 17.4 %all_to_all.16.terms_ref = bf16[4,256,512]{2,1,0:T(8,128)(2,1)S(1)} all-to-all(bf16[4,256,512]{2,1,0:T(8,128)(2,1)S(1)} %get-tuple-element.16), channel_id=1, replica_groups=mesh['dom'=128,'edge'=4] {'edge'}, dimensions={0} | all-to-all | bytes 2097152 | tf_op jit(solution)/shard_map/send_terms/all_to_all | solution.py:366
  80.3 0.0 copy-done.5
  80.3 1.4 %node_update.1 = bf16[256,512]{1,0:T(8,128)(2,1)} custom-call(bf16[4,256,512]{2,1,0:T(8,128)(2,1)S(1)} %all_to_all.16.terms_ref, bf16[256,512]{1,0:T(8,128)(2,1)S(1)} %copy-done, f32[1,512]{1,0:T(1,128)S(1)} %bitcast.13, bf16[800,512]{1,0:T(8,128)(2,1)S(1)} %get-tuple-element.10.own_w, bf16[800,512]{1,0:T(8,128)(2,1)S(1)} %collective-permute-done.near_ref.near_w, ...), custom_call_target="tpu_custom_call" | custom-call | flops 134217728 | bytes 2097152 | tf_op jit(solution)/shard_map/node_update/pallas_call | solution.py:368
  (1 shorter events, 0.0 us)
Async XLA Ops:
  3.0 21.7 %collective-permute-start = (bf16[800,512]{1,0:T(8,128)(2,1)S(1)}, bf16[800,512]{1,0:T(8,128)(2,1)S(1)}, u32[]{:S(2)}, u32[]{:S(2)}) collective-permute-start(bf16[800,512]{1,0:T(8,128)(2,1)S(1)} %get-tuple-element.10.own_w), channel_id=1, source_target_pairs={{0,1},{1,2},{2,3},{3,0},{4,7},{5,4},{6,5},{7,6},{8,9},{9,10},{10,1... | collective-permute-start | bytes 2457608 | tf_op jit(solution)/shard_map/send_near/ppermute | solution.py:318
  6.4 35.9 %all-to-all-start = ((bf16[128,16,128]{2,1,0:T(8,128)(2,1)}), bf16[128,16,128]{2,1,0:T(8,128)(2,1)}, u32[]{:S(2)}, u32[]{:S(2)}) async-start(bf16[128,16,128]{2,1,0:T(8,128)(2,1)} %bitcast.14), calls=%async_computation | async-start | bytes 1048576 | tf_op jit(solution)/shard_map/send_listed/all_to_all | solution.py:320
  24.6 3.2 %copy-start.3 = (s32[512]{0:T(512)S(1)}, s32[512]{0:T(512)}, u32[]{:S(2)}) copy-start(s32[512]{0:T(512)} %param.16) | copy-start | bytes 6148
  24.6 17.6 %copy-start = (bf16[256,512]{1,0:T(8,128)(2,1)S(1)}, bf16[256,512]{1,0:T(8,128)(2,1)}, u32[]{:S(2)}) copy-start(bf16[256,512]{1,0:T(8,128)(2,1)} %node_ref.5) | copy-start | bytes 786436
  24.7 11.2 %collective-permute-start.2 = (bf16[400,512]{1,0:T(8,128)(2,1)S(1)}, bf16[400,512]{1,0:T(8,128)(2,1)S(1)}, u32[]{:S(2)}, u32[]{:S(2)}) collective-permute-start(bf16[400,512]{1,0:T(8,128)(2,1)S(1)} %constant_dynamic-slice_fusion), channel_id=1, source_target_pairs={{0,1},{1,2},{2,3},{3,0},{4,7},{5,4},{6,5},{7,6},{8,9},{9,10},{10,1... | collective-permute-start | bytes 1228808 | tf_op jit(solution)/shard_map/send_far/ppermute | solution.py:328
  27.8 5.6 %collective-permute-start.1 = (s32[4,128]{1,0:T(4,128)S(1)}, s32[4,128]{1,0:T(4,128)S(1)}, u32[]{:S(2)}, u32[]{:S(2)}) collective-permute-start(s32[4,128]{1,0:T(4,128)S(1)} %bitcast.10), channel_id=1, source_target_pairs={{1,0},{2,1},{3,2},{0,3},{7,4},{4,5},{5,6},{6,7},{9,8},{10,9},{11,1... | collective-permute-start | bytes 6152 | tf_op jit(solution)/shard_map/send_slots/ppermute | solution.py:326
  33.4 25.5 %collective-permute-start.3 = (bf16[800,512]{1,0:T(8,128)(2,1)S(1)}, bf16[800,512]{1,0:T(8,128)(2,1)S(1)}, u32[]{:S(2)}, u32[]{:S(2)}) collective-permute-start(bf16[800,512]{1,0:T(8,128)(2,1)S(1)} %collective-permute-done.near_ref.near_w), channel_id=1, source_target_pairs={{0,4},{4,0},{8,12},{12,8},{16,20},{20,16},{24,28},{28,24},{32,36},... | collective-permute-start | bytes 2457608 | tf_op jit(solution)/shard_map/swap_near/ppermute | solution.py:331
  35.9 23.0 %collective-permute-start.4 = (bf16[400,512]{1,0:T(8,128)(2,1)S(1)}, bf16[400,512]{1,0:T(8,128)(2,1)S(1)}, u32[]{:S(2)}, u32[]{:S(2)}) collective-permute-start(bf16[400,512]{1,0:T(8,128)(2,1)S(1)} %collective-permute-done.2.far_ref.far_w), channel_id=1, source_target_pairs={{0,4},{4,0},{8,12},{12,8},{16,20},{20,16},{24,28},{28,24},{32,36},... | collective-permute-start | bytes 1228808 | tf_op jit(solution)/shard_map/swap_far/ppermute | solution.py:333
  44.9 14.0 %copy-start.1 = (bf16[512,512]{1,0:T(8,128)(2,1)S(1)}, bf16[512,512]{1,0:T(8,128)(2,1)}, u32[]{:S(2)}) copy-start(bf16[512,512]{1,0:T(8,128)(2,1)} %edge_ref.1) | copy-start | bytes 1572868
  44.9 14.0 %copy-start.2 = (bf16[128,512]{1,0:T(8,128)(2,1)S(1)}, bf16[128,512]{1,0:T(8,128)(2,1)}, u32[]{:S(2)}) copy-start(bf16[128,512]{1,0:T(8,128)(2,1)} %self_ref.1) | copy-start | bytes 393220
  58.9 0.7 copy-start.4
  62.9 17.4 %copy-start.5 = (f32[512]{0:T(512)S(1)}, f32[512]{0:T(512)}, u32[]{:S(2)}) copy-start(f32[512]{0:T(512)} %param.27) | copy-start | bytes 6148

commit v4 on v3

--- a/solution.py
+++ b/solution.py
@@ -152,7 +152,8 @@
 
 
 def choose_kernel(
-    own_ref, across_ref, near_ref, far_ref, node_ref, table_hbm, out_ref, table_ref, sem
+    own_ref, across_ref, near_ref, far_ref, node_ref, table_hbm, recv_hbm, gain_hbm,
+    out_ref, recv_ref, gain_ref, table_ref, sem,
 ):
     nodes = node_ref.shape[0]
     half = (nodes + table_hbm.shape[0]) // 2
@@ -162,7 +163,11 @@
     if split:
         parts.append((table_hbm.at[:split, :], table_ref.at[nodes:, :LANE]))
     copies = [pltpu.make_async_copy(a, b, sem.at[k]) for k, (a, b) in enumerate(parts)]
-    for c in copies:
+    ahead = [
+        pltpu.make_async_copy(recv_hbm, recv_ref, sem.at[2]),
+        pltpu.make_async_copy(gain_hbm, gain_ref, sem.at[3]),
+    ]
+    for c in copies + ahead:
         c.start()
     mine = node_ref[:, columns(lax.axis_index("edge"))]
     table_ref[: min(nodes, half), :LANE] = mine[: min(nodes, half), :]
@@ -182,33 +187,37 @@
     wanted = jnp.where(second, wanted - float(half), wanted)
     second = jnp.where(second, 1.0, 0.0)
     step = LANE if half % LANE == 0 else half
+    lane = lax.broadcasted_iota(jnp.int32, (1, step), 1).astype(F32)
+
+    def onehot_of(at):
+        place = jnp.broadcast_to(wanted[:, at : at + 1], (LANE, step))
+        return jnp.concatenate(
+            [
+                jnp.where(place == lane + float(base), 1.0, 0.0).astype(BF16)
+                for base in range(0, half, step)
+            ],
+            axis=1,
+        )
+
+    early = [onehot_of(at) for at in range(groups)]
     for c in copies:
         c.wait()
-    lane = lax.broadcasted_iota(jnp.int32, (1, step), 1).astype(F32)
     for k in range(4):
         for g in range(groups):
             at = k * groups + g
-            place = jnp.broadcast_to(wanted[:, at : at + 1], (LANE, step))
-            onehot = jnp.concatenate(
-                [
-                    jnp.where(place == lane + float(base), 1.0, 0.0).astype(BF16)
-                    for base in range(0, half, step)
-                ],
-                axis=1,
-            )
-            found = dot(onehot, table_ref[...])
+            found = dot(early[at] if at < groups else onehot_of(at), table_ref[...])
             later = jnp.broadcast_to(second[:, at : at + 1], (LANE, LANE)) > 0.5
             found = jnp.where(later, found[:, LANE:], found[:, :LANE])
             out_ref[order[k], :, g * LANE : (g + 1) * LANE] = found.astype(BF16)
+    for c in ahead:
+        c.wait()
 
 
 def edge_kernel(
-    edge_ref, node_ref, self_ref, gain_hbm, got_ref, recv_ref,
+    edge_ref, node_ref, self_ref, gain_ref, got_ref, recv_ref,
     own_w, near_w, across_w, far_w, far_across_w,
-    out_ref, term_ref, hidden_ref, message_ref, total_ref, gain_ref, sem,
+    out_hbm, term_ref, hidden_ref, message_ref, total_ref, out_ref, sem,
 ):
-    gain_in = pltpu.make_async_copy(gain_hbm, gain_ref, sem)
-    gain_in.start()
     order = shard_order()
     edges = edge_ref.shape[0]
     nodes = node_ref.shape[0]
@@ -226,10 +235,12 @@
         before = dot(by_shard(edge_ref, rows, order), w_edge) + dot(sender, w_send)
         hidden_ref[rows, :] = silu(before + dot(onehot, at_node)).astype(BF16)
     w_out = stacked(W_OUT, *shards)
-    gain_in.wait()
-    for rows in blocks:
+    copies = []
+    for g, rows in enumerate(blocks):
         message = normalize(dot(by_shard(hidden_ref, rows, order), w_out)) * gain_ref[...]
         out_ref[rows, :] = (edge_ref[rows, :].astype(F32) + message).astype(BF16)
+        copies.append(pltpu.make_async_copy(out_ref.at[rows, :], out_hbm.at[rows, :], sem.at[g]))
+        copies[-1].start()
         message_ref[rows, :] = message.astype(BF16)
     node = lax.broadcasted_iota(jnp.int32, (nodes, LANE), 0)
     onehot = jnp.concatenate(
@@ -245,22 +256,28 @@
     term = (term + dot(own, self_ref[...])).astype(BF16)
     for j in range(term_ref.shape[0]):
         term_ref[j] = term
+    for c in copies:
+        c.wait()
 
 
 def node_kernel(
     terms_ref, node_ref, gain_ref, own_w, near_w, across_w, far_w, far_across_w,
-    out_ref, hidden_ref,
+    out_hbm, hidden_ref, out_ref, sem,
 ):
     order = shard_order()
-    terms = [terms_ref[j].astype(F32) for j in range(terms_ref.shape[0])]
-    hidden_ref[...] = silu((terms[0] + terms[1]) + (terms[2] + terms[3])).astype(BF16)
-    update = normalize(
-        dot(
-            by_shard(hidden_ref, slice(None), order),
-            stacked(W_NODE, own_w, near_w, across_w, far_w, far_across_w),
-        )
-    )
-    out_ref[...] = (node_ref[...].astype(F32) + update * gain_ref[...]).astype(BF16)
+    w_node = stacked(W_NODE, own_w, near_w, across_w, far_w, far_across_w)
+    copies = []
+    for g in range(node_ref.shape[0] // LANE):
+        rows = slice(g * LANE, (g + 1) * LANE)
+        terms = [terms_ref[j, rows, :].astype(F32) for j in range(terms_ref.shape[0])]
+        hidden = silu((terms[0] + terms[1]) + (terms[2] + terms[3]))
+        hidden_ref[rows, :] = hidden.astype(BF16)
+        update = normalize(dot(by_shard(hidden_ref, rows, order), w_node))
+        out_ref[rows, :] = (node_ref[rows, :].astype(F32) + update * gain_ref[...]).astype(BF16)
+        copies.append(pltpu.make_async_copy(out_ref.at[rows, :], out_hbm.at[rows, :], sem.at[g]))
+        copies[-1].start()
+    for c in copies:
+        c.wait()
 
 
 def local(
@@ -334,44 +351,58 @@
     shards = (own_w, near_w, across_w, far_half, across_half)
 
     with jax.named_scope("choose_senders"):
-        chosen = call(
+        chosen, recv_again, gain_again = call(
             choose_kernel,
-            weight((4, LANE, groups * LANE), BF16),
-            [whole()] * 5 + [anywhere],
+            (
+                weight((4, LANE, groups * LANE), BF16),
+                pltpu.VMEM((groups, LANE), jnp.int32),
+                pltpu.VMEM((1, width), F32),
+            ),
+            [whole()] * 5 + [anywhere] * 3,
             2 * 2 * edges * entries * LANE,
             entries * LANE * 2 + 4 * edges * LANE * 2,
-            scratch=[pltpu.VMEM(((nodes + entries) // 2, 2 * LANE), BF16), dma((2,))],
-        )(own_slot, across_slot, near_w, far_half, node_feat, arrived.reshape(entries, LANE))
+            scratch=[pltpu.VMEM(((nodes + entries) // 2, 2 * LANE), BF16), dma((4,))],
+            out_specs=(whole(),) * 3,
+        )(
+            own_slot, across_slot, near_w, far_half, node_feat, arrived.reshape(entries, LANE),
+            *in_hbm(recv, edge_gain.reshape(1, width)),
+        )
     with jax.named_scope("send_senders"):
         got = lax.all_to_all(chosen, "edge", split_axis=0, concat_axis=0, tiled=True)
     with jax.named_scope("edge_update"):
         edge_out, term = call(
             edge_kernel,
-            (weight((edges, width), BF16), weight((4, nodes, hid), BF16)),
-            [whole()] * 3 + [anywhere] + [whole()] * 7,
+            (pltpu.HBM((edges, width), BF16), weight((4, nodes, hid), BF16)),
+            [whole()] * 11,
             2 * (2 * edges + 2 * nodes) * width * hid,
             edges * width * 10 + 3 * width * hid * 2,
             scratch=[
                 pltpu.VMEM((edges, hid), BF16),
                 pltpu.VMEM((edges, width), BF16),
                 pltpu.VMEM((nodes, width), BF16),
-                pltpu.VMEM((1, width), F32),
-                dma(()),
+                pltpu.VMEM((edges, width), BF16),
+                dma((groups,)),
             ],
+            out_specs=(anywhere, whole()),
         )(
-            *in_vmem(edge_feat, node_feat, node_w_self), *in_hbm(edge_gain.reshape(1, width)),
-            got, *in_vmem(recv), *shards,
+            *in_vmem(edge_feat, node_feat, node_w_self, gain_again),
+            got, *in_vmem(recv_again), *shards,
         )
     with jax.named_scope("send_terms"):
         terms = lax.all_to_all(term, "edge", split_axis=0, concat_axis=0, tiled=True)
     with jax.named_scope("node_update"):
         node_out = call(
             node_kernel,
-            weight((nodes, width), BF16),
+            pltpu.HBM((nodes, width), BF16),
             [whole()] * 8,
             2 * nodes * width * hid,
             nodes * width * 12 + width * hid * 2,
-            scratch=[pltpu.VMEM((nodes, hid), BF16)],
+            scratch=[
+                pltpu.VMEM((nodes, hid), BF16),
+                pltpu.VMEM((nodes, width), BF16),
+                dma((nodes // LANE,)),
+            ],
+            out_specs=anywhere,
         )(terms, node_feat, node_gain.reshape(1, width), *shards)
     return (node_out, edge_out)
 

time: 82.1 us -> 80.6 us (0.982)
  no operation moved by 1% of the time
where the time goes in v4:
time: 80.6 us; the launch traced here: 80.1 us
  starting transfers between devices  33.2 us (41%)
  blocking collectives  31.3 us (39%)
  Pallas kernels  8.82 us (11%)
  waiting for transfers between devices  5.94 us (7%)
    all_to_all x1, starting transfers between devices, local(): lax.all_to_all(outgoing.reshape(peers, slots, LANE), 'dom', split_axis=0,...  18.2 us
    all_to_all x1, blocking collectives, local(): lax.all_to_all(term, 'edge', split_axis=0, concat_axis=0, tiled=True)  17.4 us
    all_to_all x1, blocking collectives, local(): lax.all_to_all(chosen, 'edge', split_axis=0, concat_axis=0, tiled=True)  13.9 us
    all_to_all x1, waiting for transfers between devices, local(): lax.all_to_all(outgoing.reshape(peers, slots, LANE), 'dom', split_axis=0,...  4.43 us
    ppermute x1, starting transfers between devices, local(): across_slot = lax.ppermute(back_slot, ('dom', 'edge'), back)  4.08 us
    ppermute x1, starting transfers between devices, local(): near_w = lax.ppermute(own_w, ('dom', 'edge'), both)  3.4 us
    ppermute x1, starting transfers between devices, local(): far_half = lax.ppermute(half, ('dom', 'edge'), both)  3.1 us
    pallas_call x1, Pallas kernels, local(): call(choose_kernel, (weight((4, LANE, groups * LANE), BF16), pltpu.VMEM((...  2.63 us
  transfers between devices with their start and end apart: 6, of which 2 were waited for; matrix products, arithmetic and copies ran while one was open for 0% of the time, Pallas kernels for 3%

profile of v4, /device:TPU:56, one launch (start us, length us, event | category | flops | bytes accessed | tf_op | source)
XLA Modules:
  0.0 80.1 jit_solution(995085594262085421)
XLA Ops:
  0.6 2.3 %pick_listed.1 = (bf16[2048,128]{1,0:T(8,128)(2,1)}, bf16[800,512]{1,0:T(8,128)(2,1)S(1)}) custom-call(s32[16,128]{1,0:T(8,128)} %bitcast.16, bf16[256,512]{1,0:T(8,128)(2,1)} %node_ref.5, s32[4,128]{1,0:T(4,128)} %bitcast.10, bf16[128,512]{1,0:T(8,128)(2,1)} %refs_0_.1, bf16[128,512]{1,0:T(8,128)(2,1)} %refs_1_.1, bf16[128,512]{1,0:T(8,128)(2,1)} %refs_2_.1, ...), custom_call_target="tpu_custom_call" | custom-call | flops 335544320 | bytes 786432 | tf_op jit(solution)/shard_map/pick_listed/pallas_call | solution.py:313
  3.0 3.4 %collective-permute-start = (bf16[800,512]{1,0:T(8,128)(2,1)S(1)}, bf16[800,512]{1,0:T(8,128)(2,1)S(1)}, u32[]{:S(2)}, u32[]{:S(2)}) collective-permute-start(bf16[800,512]{1,0:T(8,128)(2,1)S(1)} %get-tuple-element.13.own_w), channel_id=1, source_target_pairs={{0,1},{1,2},{2,3},{3,0},{4,7},{5,4},{6,5},{7,6},{8,9},{9,10},{10,1... | collective-permute-start | bytes 2457608 | tf_op jit(solution)/shard_map/send_near/ppermute | solution.py:335
  6.4 18.2 %all-to-all-start = ((bf16[128,16,128]{2,1,0:T(8,128)(2,1)}), bf16[128,16,128]{2,1,0:T(8,128)(2,1)}, u32[]{:S(2)}, u32[]{:S(2)}) async-start(bf16[128,16,128]{2,1,0:T(8,128)(2,1)} %bitcast.13), calls=%async_computation | async-start | bytes 1048576 | tf_op jit(solution)/shard_map/send_listed/all_to_all | solution.py:337
  24.6 0.0 copy-start.4
  24.6 0.0 copy-start
  24.6 0.0 collective-permute-done.near_ref.near_w
  24.7 3.1 %collective-permute-start.2 = (bf16[400,512]{1,0:T(8,128)(2,1)S(1)}, bf16[400,512]{1,0:T(8,128)(2,1)S(1)}, u32[]{:S(2)}, u32[]{:S(2)}) collective-permute-start(bf16[400,512]{1,0:T(8,128)(2,1)S(1)} %constant_dynamic-slice_fusion), channel_id=1, source_target_pairs={{0,1},{1,2},{2,3},{3,0},{4,7},{5,4},{6,5},{7,6},{8,9},{9,10},{10,1... | collective-permute-start | bytes 1228808 | tf_op jit(solution)/shard_map/send_far/ppermute | solution.py:345
  27.8 0.0 copy-done.4
  27.8 4.1 %collective-permute-start.1 = (s32[4,128]{1,0:T(4,128)S(1)}, s32[4,128]{1,0:T(4,128)S(1)}, u32[]{:S(2)}, u32[]{:S(2)}) collective-permute-start(s32[4,128]{1,0:T(4,128)S(1)} %bitcast.11), channel_id=1, source_target_pairs={{1,0},{2,1},{3,2},{0,3},{7,4},{4,5},{5,6},{6,7},{9,8},{10,9},{11,1... | collective-permute-start | bytes 6152 | tf_op jit(solution)/shard_map/send_slots/ppermute | solution.py:343
  31.9 1.5 %collective-permute-done.1.across_ref = s32[4,128]{1,0:T(4,128)S(1)} collective-permute-done((s32[4,128]{1,0:T(4,128)S(1)}, s32[4,128]{1,0:T(4,128)S(1)}, u32[]{:S(2)}, u32[]{:S(2)}) %collective-permute-start.1) | collective-permute-done | bytes 2080 | tf_op jit(solution)/shard_map/send_slots/ppermute | solution.py:343
  33.4 2.5 %collective-permute-start.3 = (bf16[800,512]{1,0:T(8,128)(2,1)S(1)}, bf16[800,512]{1,0:T(8,128)(2,1)S(1)}, u32[]{:S(2)}, u32[]{:S(2)}) collective-permute-start(bf16[800,512]{1,0:T(8,128)(2,1)S(1)} %collective-permute-done.near_ref.near_w), channel_id=1, source_target_pairs={{0,4},{4,0},{8,12},{12,8},{16,20},{20,16},{24,28},{28,24},{32,36},... | collective-permute-start | bytes 2457608 | tf_op jit(solution)/shard_map/swap_near/ppermute | solution.py:348
  35.9 0.0 collective-permute-done.2.far_ref.far_w
  35.9 1.9 %collective-permute-start.4 = (bf16[400,512]{1,0:T(8,128)(2,1)S(1)}, bf16[400,512]{1,0:T(8,128)(2,1)S(1)}, u32[]{:S(2)}, u32[]{:S(2)}) collective-permute-start(bf16[400,512]{1,0:T(8,128)(2,1)S(1)} %collective-permute-done.2.far_ref.far_w), channel_id=1, source_target_pairs={{0,4},{4,0},{8,12},{12,8},{16,20},{20,16},{24,28},{28,24},{32,36},... | collective-permute-start | bytes 1228808 | tf_op jit(solution)/shard_map/swap_far/ppermute | solution.py:350
  37.8 4.4 %all-to-all-done = bf16[128,16,128]{2,1,0:T(8,128)(2,1)} async-done(((bf16[128,16,128]{2,1,0:T(8,128)(2,1)}), bf16[128,16,128]{2,1,0:T(8,128)(2,1)}, u32[]{:S(2)}, u32[]{:S(2)}) %all-to-all-start) | async-done | bytes 524320 | tf_op jit(solution)/shard_map/send_listed/all_to_all | solution.py:337
  42.3 0.0 copy-done
  42.3 2.6 %choose_senders.1 = (bf16[4,128,512]{2,1,0:T(8,128)(2,1)S(1)}, s32[4,128]{1,0:T(4,128)S(1)}, f32[1,512]{1,0:T(1,128)S(1)}) custom-call(s32[4,128]{1,0:T(4,128)S(1)} %bitcast.12, s32[4,128]{1,0:T(4,128)S(1)} %collective-permute-done.1.across_ref, bf16[800,512]{1,0:T(8,128)(2,1)S(1)} %collective-permute-done.near_ref.near_w, ...), custom_call_target="tpu_custom_call" | custom-call | flops 536870912 | bytes 1048576 | tf_op jit(solution)/shard_map/choose_senders/pallas_call | solution.py:354
  44.9 0.0 copy-start.1
  44.9 0.0 copy-start.2
  44.9 13.9 %all_to_all.15.got_ref = bf16[4,128,512]{2,1,0:T(8,128)(2,1)S(1)} all-to-all(bf16[4,128,512]{2,1,0:T(8,128)(2,1)S(1)} %get-tuple-element.19), channel_id=1, replica_groups=mesh['dom'=128,'edge'=4] {'edge'}, dimensions={0} | all-to-all | bytes 1048576 | tf_op jit(solution)/shard_map/send_senders/all_to_all | solution.py:371
  58.9 0.0 collective-permute-done.4.far_across_w
  58.9 0.0 collective-permute-done.3.across_w
  58.9 0.0 copy-done.1
  58.9 0.0 copy-done.2
  58.9 2.6 %edge_update.1 = (bf16[512,512]{1,0:T(8,128)(2,1)}, bf16[4,256,512]{2,1,0:T(8,128)(2,1)S(1)}) custom-call(bf16[512,512]{1,0:T(8,128)(2,1)S(1)} %copy-done.1, bf16[256,512]{1,0:T(8,128)(2,1)S(1)} %copy-done, bf16[128,512]{1,0:T(8,128)(2,1)S(1)} %copy-done.2, f32[1,512]{1,0:T(1,128)S(1)} %get-tuple-element.18.gain_ref, ...), custom_call_target="tpu_custom_call" | custom-call | flops 805306368 | bytes 4194304 | tf_op jit(solution)/shard_map/edge_update/pallas_call | solution.py:373
  61.5 0.0 copy-start.3
  61.5 17.4 %all_to_all.16.terms_ref = bf16[4,256,512]{2,1,0:T(8,128)(2,1)S(1)} all-to-all(bf16[4,256,512]{2,1,0:T(8,128)(2,1)S(1)} %get-tuple-element.22), channel_id=1, replica_groups=mesh['dom'=128,'edge'=4] {'edge'}, dimensions={0} | all-to-all | bytes 2097152 | tf_op jit(solution)/shard_map/send_terms/all_to_all | solution.py:392
  78.8 0.0 copy-done.3
  78.8 1.3 %node_update.1 = bf16[256,512]{1,0:T(8,128)(2,1)} custom-call(bf16[4,256,512]{2,1,0:T(8,128)(2,1)S(1)} %all_to_all.16.terms_ref, bf16[256,512]{1,0:T(8,128)(2,1)S(1)} %copy-done, f32[1,512]{1,0:T(1,128)S(1)} %bitcast.9, bf16[800,512]{1,0:T(8,128)(2,1)S(1)} %get-tuple-element.13.own_w, bf16[800,512]{1,0:T(8,128)(2,1)S(1)} %collective-permute-done.near_ref.near_w, ...), custom_call_target="tpu_custom_call" | custom-call | flops 134217728 | bytes 2097152 | tf_op jit(solution)/shard_map/node_update/pallas_call | solution.py:394
  (1 shorter events, 0.0 us)
Async XLA Ops:
  3.0 21.7 %collective-permute-start = (bf16[800,512]{1,0:T(8,128)(2,1)S(1)}, bf16[800,512]{1,0:T(8,128)(2,1)S(1)}, u32[]{:S(2)}, u32[]{:S(2)}) collective-permute-start(bf16[800,512]{1,0:T(8,128)(2,1)S(1)} %get-tuple-element.13.own_w), channel_id=1, source_target_pairs={{0,1},{1,2},{2,3},{3,0},{4,7},{5,4},{6,5},{7,6},{8,9},{9,10},{10,1... | collective-permute-start | bytes 2457608 | tf_op jit(solution)/shard_map/send_near/ppermute | solution.py:335
  6.4 35.9 %all-to-all-start = ((bf16[128,16,128]{2,1,0:T(8,128)(2,1)}), bf16[128,16,128]{2,1,0:T(8,128)(2,1)}, u32[]{:S(2)}, u32[]{:S(2)}) async-start(bf16[128,16,128]{2,1,0:T(8,128)(2,1)} %bitcast.13), calls=%async_computation | async-start | bytes 1048576 | tf_op jit(solution)/shard_map/send_listed/all_to_all | solution.py:337
  24.6 3.2 %copy-start.4 = (s32[512]{0:T(512)S(1)}, s32[512]{0:T(512)}, u32[]{:S(2)}) copy-start(s32[512]{0:T(512)} %param.16) | copy-start | bytes 6148
  24.6 17.6 %copy-start = (bf16[256,512]{1,0:T(8,128)(2,1)S(1)}, bf16[256,512]{1,0:T(8,128)(2,1)}, u32[]{:S(2)}) copy-start(bf16[256,512]{1,0:T(8,128)(2,1)} %node_ref.5) | copy-start | bytes 786436
  24.7 11.2 %collective-permute-start.2 = (bf16[400,512]{1,0:T(8,128)(2,1)S(1)}, bf16[400,512]{1,0:T(8,128)(2,1)S(1)}, u32[]{:S(2)}, u32[]{:S(2)}) collective-permute-start(bf16[400,512]{1,0:T(8,128)(2,1)S(1)} %constant_dynamic-slice_fusion), channel_id=1, source_target_pairs={{0,1},{1,2},{2,3},{3,0},{4,7},{5,4},{6,5},{7,6},{8,9},{9,10},{10,1... | collective-permute-start | bytes 1228808 | tf_op jit(solution)/shard_map/send_far/ppermute | solution.py:345
  27.8 5.6 %collective-permute-start.1 = (s32[4,128]{1,0:T(4,128)S(1)}, s32[4,128]{1,0:T(4,128)S(1)}, u32[]{:S(2)}, u32[]{:S(2)}) collective-permute-start(s32[4,128]{1,0:T(4,128)S(1)} %bitcast.11), channel_id=1, source_target_pairs={{1,0},{2,1},{3,2},{0,3},{7,4},{4,5},{5,6},{6,7},{9,8},{10,9},{11,1... | collective-permute-start | bytes 6152 | tf_op jit(solution)/shard_map/send_slots/ppermute | solution.py:343
  33.4 25.5 %collective-permute-start.3 = (bf16[800,512]{1,0:T(8,128)(2,1)S(1)}, bf16[800,512]{1,0:T(8,128)(2,1)S(1)}, u32[]{:S(2)}, u32[]{:S(2)}) collective-permute-start(bf16[800,512]{1,0:T(8,128)(2,1)S(1)} %collective-permute-done.near_ref.near_w), channel_id=1, source_target_pairs={{0,4},{4,0},{8,12},{12,8},{16,20},{20,16},{24,28},{28,24},{32,36},... | collective-permute-start | bytes 2457608 | tf_op jit(solution)/shard_map/swap_near/ppermute | solution.py:348
  35.9 22.9 %collective-permute-start.4 = (bf16[400,512]{1,0:T(8,128)(2,1)S(1)}, bf16[400,512]{1,0:T(8,128)(2,1)S(1)}, u32[]{:S(2)}, u32[]{:S(2)}) collective-permute-start(bf16[400,512]{1,0:T(8,128)(2,1)S(1)} %collective-permute-done.2.far_ref.far_w), channel_id=1, source_target_pairs={{0,4},{4,0},{8,12},{12,8},{16,20},{20,16},{24,28},{28,24},{32,36},... | collective-permute-start | bytes 1228808 | tf_op jit(solution)/shard_map/swap_far/ppermute | solution.py:350
  44.9 14.0 %copy-start.1 = (bf16[512,512]{1,0:T(8,128)(2,1)S(1)}, bf16[512,512]{1,0:T(8,128)(2,1)}, u32[]{:S(2)}) copy-start(bf16[512,512]{1,0:T(8,128)(2,1)} %edge_ref.1) | copy-start | bytes 1572868
  44.9 14.0 %copy-start.2 = (bf16[128,512]{1,0:T(8,128)(2,1)S(1)}, bf16[128,512]{1,0:T(8,128)(2,1)}, u32[]{:S(2)}) copy-start(bf16[128,512]{1,0:T(8,128)(2,1)} %self_ref.1) | copy-start | bytes 393220
  61.5 17.4 %copy-start.3 = (f32[512]{0:T(512)S(1)}, f32[512]{0:T(512)}, u32[]{:S(2)}) copy-start(f32[512]{0:T(512)} %param.27) | copy-start | bytes 6148

commit v5 on v4

--- a/solution.py
+++ b/solution.py
@@ -107,7 +107,7 @@
     first[0].wait()
     listed = column_of(listed_ref[...])
     first[1].wait()
-    chunk = min(32, peers)
+    chunk = min(64, peers)
     rows = chunk * slots
     for k, peer in enumerate(range(0, peers, chunk)):
         at = peer * slots
@@ -320,7 +320,7 @@
                 pltpu.VMEM((slots, peers), jnp.int32),
                 pltpu.VMEM((nodes, LANE), BF16),
                 pltpu.VMEM((groups, LANE), jnp.int32),
-                pltpu.VMEM((entries, LANE), F32),
+                pltpu.VMEM((entries + slots, LANE), F32),
                 pltpu.VMEM((entries, LANE), BF16),
                 dma((9 + max(1, peers // 32),)),
             ],

time: 80.6 us -> 80.6 us (level)
  no operation moved by 1% of the time
where the time goes in v5:
time: 80.6 us; the launch traced here: 80.2 us
  starting transfers between devices  33.2 us (41%)
  blocking collectives  31.3 us (39%)
  Pallas kernels  8.86 us (11%)
  waiting for transfers between devices  5.94 us (7%)
    all_to_all x1, starting transfers between devices, local(): lax.all_to_all(outgoing.reshape(peers, slots, LANE), 'dom', split_axis=0,...  18.2 us
    all_to_all x1, blocking collectives, local(): lax.all_to_all(term, 'edge', split_axis=0, concat_axis=0, tiled=True)  17.4 us
    all_to_all x1, blocking collectives, local(): lax.all_to_all(chosen, 'edge', split_axis=0, concat_axis=0, tiled=True)  13.9 us
    all_to_all x1, waiting for transfers between devices, local(): lax.all_to_all(outgoing.reshape(peers, slots, LANE), 'dom', split_axis=0,...  4.43 us
    ppermute x1, starting transfers between devices, local(): across_slot = lax.ppermute(back_slot, ('dom', 'edge'), back)  4.08 us
    ppermute x1, starting transfers between devices, local(): near_w = lax.ppermute(own_w, ('dom', 'edge'), both)  3.4 us
    ppermute x1, starting transfers between devices, local(): far_half = lax.ppermute(half, ('dom', 'edge'), both)  3.1 us
    pallas_call x1, Pallas kernels, local(): call(choose_kernel, (weight((4, LANE, groups * LANE), BF16), pltpu.VMEM((...  2.63 us
  transfers between devices with their start and end apart: 6, of which 2 were waited for; matrix products, arithmetic and copies ran while one was open for 0% of the time, Pallas kernels for 3%

profile of v5, /device:TPU:56, one launch (start us, length us, event | category | flops | bytes accessed | tf_op | source)
XLA Modules:
  0.0 80.2 jit_solution(14875561326180069450)
XLA Ops:
  0.6 2.4 %pick_listed.1 = (bf16[2048,128]{1,0:T(8,128)(2,1)}, bf16[800,512]{1,0:T(8,128)(2,1)S(1)}) custom-call(s32[16,128]{1,0:T(8,128)} %bitcast.16, bf16[256,512]{1,0:T(8,128)(2,1)} %node_ref.5, s32[4,128]{1,0:T(4,128)} %bitcast.10, bf16[128,512]{1,0:T(8,128)(2,1)} %refs_0_.1, bf16[128,512]{1,0:T(8,128)(2,1)} %refs_1_.1, bf16[128,512]{1,0:T(8,128)(2,1)} %refs_2_.1, ...), custom_call_target="tpu_custom_call" | custom-call | flops 335544320 | bytes 786432 | tf_op jit(solution)/shard_map/pick_listed/pallas_call | solution.py:313
  3.0 3.4 %collective-permute-start = (bf16[800,512]{1,0:T(8,128)(2,1)S(1)}, bf16[800,512]{1,0:T(8,128)(2,1)S(1)}, u32[]{:S(2)}, u32[]{:S(2)}) collective-permute-start(bf16[800,512]{1,0:T(8,128)(2,1)S(1)} %get-tuple-element.13.own_w), channel_id=1, source_target_pairs={{0,1},{1,2},{2,3},{3,0},{4,7},{5,4},{6,5},{7,6},{8,9},{9,10},{10,1... | collective-permute-start | bytes 2457608 | tf_op jit(solution)/shard_map/send_near/ppermute | solution.py:335
  6.4 18.2 %all-to-all-start = ((bf16[128,16,128]{2,1,0:T(8,128)(2,1)}), bf16[128,16,128]{2,1,0:T(8,128)(2,1)}, u32[]{:S(2)}, u32[]{:S(2)}) async-start(bf16[128,16,128]{2,1,0:T(8,128)(2,1)} %bitcast.13), calls=%async_computation | async-start | bytes 1048576 | tf_op jit(solution)/shard_map/send_listed/all_to_all | solution.py:337
  24.7 0.0 copy-start.4
  24.7 0.0 copy-start
  24.7 0.0 collective-permute-done.near_ref.near_w
  24.7 3.1 %collective-permute-start.2 = (bf16[400,512]{1,0:T(8,128)(2,1)S(1)}, bf16[400,512]{1,0:T(8,128)(2,1)S(1)}, u32[]{:S(2)}, u32[]{:S(2)}) collective-permute-start(bf16[400,512]{1,0:T(8,128)(2,1)S(1)} %constant_dynamic-slice_fusion), channel_id=1, source_target_pairs={{0,1},{1,2},{2,3},{3,0},{4,7},{5,4},{6,5},{7,6},{8,9},{9,10},{10,1... | collective-permute-start | bytes 1228808 | tf_op jit(solution)/shard_map/send_far/ppermute | solution.py:345
  27.8 0.0 copy-done.4
  27.9 4.1 %collective-permute-start.1 = (s32[4,128]{1,0:T(4,128)S(1)}, s32[4,128]{1,0:T(4,128)S(1)}, u32[]{:S(2)}, u32[]{:S(2)}) collective-permute-start(s32[4,128]{1,0:T(4,128)S(1)} %bitcast.11), channel_id=1, source_target_pairs={{1,0},{2,1},{3,2},{0,3},{7,4},{4,5},{5,6},{6,7},{9,8},{10,9},{11,1... | collective-permute-start | bytes 6152 | tf_op jit(solution)/shard_map/send_slots/ppermute | solution.py:343
  31.9 1.5 %collective-permute-done.1.across_ref = s32[4,128]{1,0:T(4,128)S(1)} collective-permute-done((s32[4,128]{1,0:T(4,128)S(1)}, s32[4,128]{1,0:T(4,128)S(1)}, u32[]{:S(2)}, u32[]{:S(2)}) %collective-permute-start.1) | collective-permute-done | bytes 2080 | tf_op jit(solution)/shard_map/send_slots/ppermute | solution.py:343
  33.4 2.5 %collective-permute-start.3 = (bf16[800,512]{1,0:T(8,128)(2,1)S(1)}, bf16[800,512]{1,0:T(8,128)(2,1)S(1)}, u32[]{:S(2)}, u32[]{:S(2)}) collective-permute-start(bf16[800,512]{1,0:T(8,128)(2,1)S(1)} %collective-permute-done.near_ref.near_w), channel_id=1, source_target_pairs={{0,4},{4,0},{8,12},{12,8},{16,20},{20,16},{24,28},{28,24},{32,36},... | collective-permute-start | bytes 2457608 | tf_op jit(solution)/shard_map/swap_near/ppermute | solution.py:348
  35.9 0.0 collective-permute-done.2.far_ref.far_w
  35.9 1.9 %collective-permute-start.4 = (bf16[400,512]{1,0:T(8,128)(2,1)S(1)}, bf16[400,512]{1,0:T(8,128)(2,1)S(1)}, u32[]{:S(2)}, u32[]{:S(2)}) collective-permute-start(bf16[400,512]{1,0:T(8,128)(2,1)S(1)} %collective-permute-done.2.far_ref.far_w), channel_id=1, source_target_pairs={{0,4},{4,0},{8,12},{12,8},{16,20},{20,16},{24,28},{28,24},{32,36},... | collective-permute-start | bytes 1228808 | tf_op jit(solution)/shard_map/swap_far/ppermute | solution.py:350
  37.9 4.4 %all-to-all-done = bf16[128,16,128]{2,1,0:T(8,128)(2,1)} async-done(((bf16[128,16,128]{2,1,0:T(8,128)(2,1)}), bf16[128,16,128]{2,1,0:T(8,128)(2,1)}, u32[]{:S(2)}, u32[]{:S(2)}) %all-to-all-start) | async-done | bytes 524320 | tf_op jit(solution)/shard_map/send_listed/all_to_all | solution.py:337
  42.3 0.0 copy-done
  42.3 2.6 %choose_senders.1 = (bf16[4,128,512]{2,1,0:T(8,128)(2,1)S(1)}, s32[4,128]{1,0:T(4,128)S(1)}, f32[1,512]{1,0:T(1,128)S(1)}) custom-call(s32[4,128]{1,0:T(4,128)S(1)} %bitcast.12, s32[4,128]{1,0:T(4,128)S(1)} %collective-permute-done.1.across_ref, bf16[800,512]{1,0:T(8,128)(2,1)S(1)} %collective-permute-done.near_ref.near_w, ...), custom_call_target="tpu_custom_call" | custom-call | flops 536870912 | bytes 1048576 | tf_op jit(solution)/shard_map/choose_senders/pallas_call | solution.py:354
  44.9 0.0 copy-start.1
  44.9 0.0 copy-start.2
  45.0 13.9 %all_to_all.15.got_ref = bf16[4,128,512]{2,1,0:T(8,128)(2,1)S(1)} all-to-all(bf16[4,128,512]{2,1,0:T(8,128)(2,1)S(1)} %get-tuple-element.19), channel_id=1, replica_groups=mesh['dom'=128,'edge'=4] {'edge'}, dimensions={0} | all-to-all | bytes 1048576 | tf_op jit(solution)/shard_map/send_senders/all_to_all | solution.py:371
  58.9 0.0 collective-permute-done.4.far_across_w
  58.9 0.0 collective-permute-done.3.across_w
  58.9 0.0 copy-done.1
  58.9 0.0 copy-done.2
  58.9 2.6 %edge_update.1 = (bf16[512,512]{1,0:T(8,128)(2,1)}, bf16[4,256,512]{2,1,0:T(8,128)(2,1)S(1)}) custom-call(bf16[512,512]{1,0:T(8,128)(2,1)S(1)} %copy-done.1, bf16[256,512]{1,0:T(8,128)(2,1)S(1)} %copy-done, bf16[128,512]{1,0:T(8,128)(2,1)S(1)} %copy-done.2, f32[1,512]{1,0:T(1,128)S(1)} %get-tuple-element.18.gain_ref, ...), custom_call_target="tpu_custom_call" | custom-call | flops 805306368 | bytes 4194304 | tf_op jit(solution)/shard_map/edge_update/pallas_call | solution.py:373
  61.5 0.0 copy-start.3
  61.5 17.4 %all_to_all.16.terms_ref = bf16[4,256,512]{2,1,0:T(8,128)(2,1)S(1)} all-to-all(bf16[4,256,512]{2,1,0:T(8,128)(2,1)S(1)} %get-tuple-element.22), channel_id=1, replica_groups=mesh['dom'=128,'edge'=4] {'edge'}, dimensions={0} | all-to-all | bytes 2097152 | tf_op jit(solution)/shard_map/send_terms/all_to_all | solution.py:392
  78.9 0.0 copy-done.3
  78.9 1.3 %node_update.1 = bf16[256,512]{1,0:T(8,128)(2,1)} custom-call(bf16[4,256,512]{2,1,0:T(8,128)(2,1)S(1)} %all_to_all.16.terms_ref, bf16[256,512]{1,0:T(8,128)(2,1)S(1)} %copy-done, f32[1,512]{1,0:T(1,128)S(1)} %bitcast.9, bf16[800,512]{1,0:T(8,128)(2,1)S(1)} %get-tuple-element.13.own_w, bf16[800,512]{1,0:T(8,128)(2,1)S(1)} %collective-permute-done.near_ref.near_w, ...), custom_call_target="tpu_custom_call" | custom-call | flops 134217728 | bytes 2097152 | tf_op jit(solution)/shard_map/node_update/pallas_call | solution.py:394
  (1 shorter events, 0.0 us)
Async XLA Ops:
  3.0 21.7 %collective-permute-start = (bf16[800,512]{1,0:T(8,128)(2,1)S(1)}, bf16[800,512]{1,0:T(8,128)(2,1)S(1)}, u32[]{:S(2)}, u32[]{:S(2)}) collective-permute-start(bf16[800,512]{1,0:T(8,128)(2,1)S(1)} %get-tuple-element.13.own_w), channel_id=1, source_target_pairs={{0,1},{1,2},{2,3},{3,0},{4,7},{5,4},{6,5},{7,6},{8,9},{9,10},{10,1... | collective-permute-start | bytes 2457608 | tf_op jit(solution)/shard_map/send_near/ppermute | solution.py:335
  6.4 35.9 %all-to-all-start = ((bf16[128,16,128]{2,1,0:T(8,128)(2,1)}), bf16[128,16,128]{2,1,0:T(8,128)(2,1)}, u32[]{:S(2)}, u32[]{:S(2)}) async-start(bf16[128,16,128]{2,1,0:T(8,128)(2,1)} %bitcast.13), calls=%async_computation | async-start | bytes 1048576 | tf_op jit(solution)/shard_map/send_listed/all_to_all | solution.py:337
  24.7 3.2 %copy-start.4 = (s32[512]{0:T(512)S(1)}, s32[512]{0:T(512)}, u32[]{:S(2)}) copy-start(s32[512]{0:T(512)} %param.16) | copy-start | bytes 6148
  24.7 17.6 %copy-start = (bf16[256,512]{1,0:T(8,128)(2,1)S(1)}, bf16[256,512]{1,0:T(8,128)(2,1)}, u32[]{:S(2)}) copy-start(bf16[256,512]{1,0:T(8,128)(2,1)} %node_ref.5) | copy-start | bytes 786436
  24.7 11.2 %collective-permute-start.2 = (bf16[400,512]{1,0:T(8,128)(2,1)S(1)}, bf16[400,512]{1,0:T(8,128)(2,1)S(1)}, u32[]{:S(2)}, u32[]{:S(2)}) collective-permute-start(bf16[400,512]{1,0:T(8,128)(2,1)S(1)} %constant_dynamic-slice_fusion), channel_id=1, source_target_pairs={{0,1},{1,2},{2,3},{3,0},{4,7},{5,4},{6,5},{7,6},{8,9},{9,10},{10,1... | collective-permute-start | bytes 1228808 | tf_op jit(solution)/shard_map/send_far/ppermute | solution.py:345
  27.9 5.6 %collective-permute-start.1 = (s32[4,128]{1,0:T(4,128)S(1)}, s32[4,128]{1,0:T(4,128)S(1)}, u32[]{:S(2)}, u32[]{:S(2)}) collective-permute-start(s32[4,128]{1,0:T(4,128)S(1)} %bitcast.11), channel_id=1, source_target_pairs={{1,0},{2,1},{3,2},{0,3},{7,4},{4,5},{5,6},{6,7},{9,8},{10,9},{11,1... | collective-permute-start | bytes 6152 | tf_op jit(solution)/shard_map/send_slots/ppermute | solution.py:343
  33.4 25.5 %collective-permute-start.3 = (bf16[800,512]{1,0:T(8,128)(2,1)S(1)}, bf16[800,512]{1,0:T(8,128)(2,1)S(1)}, u32[]{:S(2)}, u32[]{:S(2)}) collective-permute-start(bf16[800,512]{1,0:T(8,128)(2,1)S(1)} %collective-permute-done.near_ref.near_w), channel_id=1, source_target_pairs={{0,4},{4,0},{8,12},{12,8},{16,20},{20,16},{24,28},{28,24},{32,36},... | collective-permute-start | bytes 2457608 | tf_op jit(solution)/shard_map/swap_near/ppermute | solution.py:348
  35.9 22.9 %collective-permute-start.4 = (bf16[400,512]{1,0:T(8,128)(2,1)S(1)}, bf16[400,512]{1,0:T(8,128)(2,1)S(1)}, u32[]{:S(2)}, u32[]{:S(2)}) collective-permute-start(bf16[400,512]{1,0:T(8,128)(2,1)S(1)} %collective-permute-done.2.far_ref.far_w), channel_id=1, source_target_pairs={{0,4},{4,0},{8,12},{12,8},{16,20},{20,16},{24,28},{28,24},{32,36},... | collective-permute-start | bytes 1228808 | tf_op jit(solution)/shard_map/swap_far/ppermute | solution.py:350
  44.9 14.0 %copy-start.1 = (bf16[512,512]{1,0:T(8,128)(2,1)S(1)}, bf16[512,512]{1,0:T(8,128)(2,1)}, u32[]{:S(2)}) copy-start(bf16[512,512]{1,0:T(8,128)(2,1)} %edge_ref.1) | copy-start | bytes 1572868
  44.9 14.0 %copy-start.2 = (bf16[128,512]{1,0:T(8,128)(2,1)S(1)}, bf16[128,512]{1,0:T(8,128)(2,1)}, u32[]{:S(2)}) copy-start(bf16[128,512]{1,0:T(8,128)(2,1)} %self_ref.1) | copy-start | bytes 393220
  61.5 17.4 %copy-start.3 = (f32[512]{0:T(512)S(1)}, f32[512]{0:T(512)}, u32[]{:S(2)}) copy-start(f32[512]{0:T(512)} %param.27) | copy-start | bytes 6148
